TPU v7x, 256 devices: a whole 4x4x8 slice. The times are simulated.
256 devices in a mesh: clip: 4 (over x), seq: 16 (over z, core), split: 4 (over y).
Axes of the slice: x: 4, y: 4, z: 8, core: 2. Of those that a mesh axis runs over, the one named last changes fastest.
Arguments:
- queries: bfloat16 [32768, 4096], P(('clip', 'seq', 'split')), parts along dimension 0, may hold values from -40 to 40
- keys: bfloat16 [32768, 4096], P(('clip', 'seq', 'split')), parts along dimension 0, may hold values from -40 to 40
- values: bfloat16 [32768, 4096], P(('clip', 'seq', 'split')), parts along dimension 0, may hold values from -6 to 6
- key_blocks: int32 [128, 64, 64], P('clip'), parts along dimension 0, may hold values from 0 to 63, as said below
- block_counts: int32 [128, 64], P('clip'), parts along dimension 0, may hold values from 1 to 64, as said below
Outputs:
- attended: bfloat16 [32768, 4096], P(('clip', 'seq', 'split')), parts along dimension 0
There are 4 independent parts, one for each index of `clip`. A program takes and returns all parts, laid end to end along the dimension named above; each array names one. Nothing has to cross between parts.
Inputs may be any that keep to these rules, and one draw needn't show every extreme that they name: `key_blocks`: entry 0 of every list is the query block itself; the entries of one list are distinct; entries past block_counts are not used. `block_counts`: some heads use all 64 entries in every query block.
All inputs are finite; a program needn't handle non-finite values.
Results may differ from a plain program's by a relative error of at most 0.0044.
Values may be sent and summed in bfloat16 or wider, within the bound.
No kernel may reach another device: no remote copies, remote signals or barrier semaphores. Data moves between devices by JAX's collectives and lax.ppermute only.
A program may use at most 128 MiB of HBM per device.

v0:
```python
import jax
import jax.numpy as jnp
from jax import lax
from jax.sharding import PartitionSpec as P

HEAD_DIM = 128
BLOCK = 128


slot_group = 4


def needed(counts):
    return (jnp.max(counts) + slot_group - 1) // slot_group


def attend(q_blocks, k_head, v_head, lists, counts, bound, scale):
    nrows = q_blocks.shape[0]
    width = q_blocks.shape[1]

    def scored(turn):
        first = turn * slot_group
        picked = lax.dynamic_slice_in_dim(lists, first, slot_group, 1)
        k_group = jnp.take(k_head, picked, axis=0)
        score = (
            jnp.einsum("qbd,qjkd->qbjk", q_blocks, k_group, preferred_element_type=jnp.float32)
            * scale
        )
        slot_ids = first + jnp.arange(slot_group, dtype=jnp.int32)
        usable = slot_ids[None, :] < counts[:, None]
        return (jnp.where(usable[:, None, :, None], score, -jnp.inf), picked)

    def highest(turn, running):
        score, picked = scored(turn)
        return jnp.maximum(running, jnp.max(score, axis=(2, 3)))

    start = jnp.full((nrows, width), -jnp.inf, jnp.float32)
    running = lax.fori_loop(0, bound, highest, start)

    def accumulate(turn, carry):
        total, summed = carry
        score, picked = scored(turn)
        expo = jnp.exp(score - running[:, :, None, None])
        v_group = jnp.take(v_head, picked, axis=0)
        total = total + jnp.sum(expo, axis=(2, 3))
        summed = summed + jnp.einsum(
            "qbjk,qjkd->qbd", expo.astype(jnp.bfloat16), v_group, preferred_element_type=jnp.float32
        )
        return (total, summed)

    zero_total = jnp.zeros((nrows, width), jnp.float32)
    zero_summed = jnp.zeros((nrows, width, k_head.shape[2]), jnp.float32)
    total, summed = lax.fori_loop(0, bound, accumulate, (zero_total, zero_summed))
    safe = jnp.where(total > 0, total, 1.0)
    return (summed / safe[:, :, None]).astype(jnp.bfloat16)


def body(queries, keys, values, key_blocks, block_counts):
    seq_count = lax.axis_size("seq")
    split_count = lax.axis_size("split")
    tok_rows = queries.shape[0]
    head_dim = HEAD_DIM
    heads = queries.shape[1] // head_dim
    owned = heads // seq_count
    block = BLOCK
    blocks_dev = tok_rows // block
    seq_place = lax.axis_index("seq")
    split_place = lax.axis_index("split")
    scale = head_dim ** (-0.5)
    head_order = jnp.arange(heads, dtype=jnp.int32)
    q_ready, k_ready, v_ready = (queries, keys, values)
    q_here, k_here, v_here = (
        lax.all_to_all(q_ready, "seq", split_axis=1, concat_axis=0, tiled=True),
        lax.all_to_all(k_ready, "seq", split_axis=1, concat_axis=0, tiled=True),
        lax.all_to_all(v_ready, "seq", split_axis=1, concat_axis=0, tiled=True),
    )
    k_whole, v_whole = (
        lax.all_gather(k_here, "split", axis=0, tiled=True),
        lax.all_gather(v_here, "split", axis=0, tiled=True),
    )
    query_blocks = seq_count * blocks_dev
    key_total = k_whole.shape[0] // block
    q_four = q_here.reshape(query_blocks, block, owned, head_dim)
    k_four = k_whole.reshape(key_total, block, owned, head_dim)
    v_four = v_whole.reshape(key_total, block, owned, head_dim)
    local_index = jnp.arange(query_blocks, dtype=jnp.int32)
    query_global = (
        local_index // blocks_dev * split_count + split_place
    ) * blocks_dev + local_index % blocks_dev
    owner_heads = head_order.reshape(seq_count, owned)
    mine = jnp.take(owner_heads, seq_place, axis=0)
    global_block = jnp.take(jnp.take(key_blocks, mine, axis=0), query_global, axis=1)
    source = global_block // blocks_dev
    inner = global_block % blocks_dev
    seq_source = source // split_count
    split_source = source % split_count
    lists_mine = split_source * (seq_count * blocks_dev) + seq_source * blocks_dev + inner
    counts_mine = jnp.take(jnp.take(block_counts, mine, axis=0), query_global, axis=1)

    def whole_head(packed):
        head_place, lists, counts = packed
        q_head = jnp.take(q_four, head_place, axis=2)
        k_head = jnp.take(k_four, head_place, axis=2)
        v_head = jnp.take(v_four, head_place, axis=2)
        return attend(q_head, k_head, v_head, lists, counts, needed(counts), scale)

    outputs = lax.map(whole_head, (jnp.arange(owned, dtype=jnp.int32), lists_mine, counts_mine))
    outputs = outputs.transpose(1, 2, 0, 3).reshape(query_blocks * block, owned * head_dim)
    returned = lax.all_to_all(outputs, "seq", split_axis=0, concat_axis=1, tiled=True)
    return returned


def solution(mesh):
    in_specs = (
        P(("clip", "seq", "split"), None),
        P(("clip", "seq", "split"), None),
        P(("clip", "seq", "split"), None),
        P("clip", None, None),
        P("clip", None),
    )
    out_specs = P(("clip", "seq", "split"), None)
    return jax.shard_map(body, mesh=mesh, in_specs=in_specs, out_specs=out_specs, check_vma=False)
```

profile of v0, /device:TPU:12, one launch (start us, length us, event | category | flops | bytes accessed | tf_op | source)
XLA Modules:
  0.0 911.9 jit_solution(9155894856751514106)
XLA Ops:
  8.2 35.6 %all_to_all.73 = bf16[128,16,256]{0,2,1:T(8,128)(2,1)S(1)} all-to-all(bf16[128,16,256]{0,2,1:T(8,128)(2,1)S(1)} %bitcast.113), channel_id=1, replica_groups=mesh['clip'=4,'seq'=16,'split'=4] {'seq'}, dimensions={1} | all-to-all | bytes 2097152 | tf_op jit(solution)/shard_map/all_to_all | solution.py:74
  46.9 31.3 %all_to_all.74 = bf16[128,16,256]{0,2,1:T(8,128)(2,1)S(1)} all-to-all(bf16[128,16,256]{0,2,1:T(8,128)(2,1)S(1)} %bitcast.114), channel_id=1, replica_groups=mesh['clip'=4,'seq'=16,'split'=4] {'seq'}, dimensions={1} | all-to-all | bytes 2097152 | tf_op jit(solution)/shard_map/all_to_all | solution.py:75
  88.2 5.8 all-gather.3.cloned.1.call-done
  94.0 6.9 reshape.368
  100.9 5.3 copy.33
  106.2 40.9 %all-gather.5.cloned.1.call-done = bf16[8192,256]{1,0:T(8,128)(2,1)} async-done(((bf16[2048,256]{1,0:T(8,128)(2,1)}), bf16[8192,256]{1,0:T(8,128)(2,1)}) %all-gather.5.cloned.1.call-update) | async-done | bytes 4194320 | tf_op jit(solution)/shard_map/all_gather | solution.py:79
  147.1 6.9 reshape.369
  154.0 5.3 copy.35
  159.2 393.8 %while.91 = (s32[]{:T(128)}, bf16[2,16,128,128]{2,3,0,1:T(8,128)(2,1)}, s32[2,16]{1,0:T(2,128)S(1)}, s32[2,16,64]{2,0,1:T(2,128)S(1)}, s32[2]{0:T(128)S(1)}, /*i...) while((s32[]{:T(128)}, ...), condition=%wide.region_8.11_spmd, body=%wide.region_0.10_spmd.sunk | while | flops 823139200 | bytes 55194912 | solution.py:107
  172.8 4.8 while.92
  178.8 16.2 %while.93 = (s32[]{:T(128)}, f32[16,128]{1,0:T(8,128)S(1)}, f32[16,128,128]{2,1,0:T(8,128)}, s32[]{:T(128)}, s32[16]{0:T(128)S(1)}, /*index=5*/s32[16,64]{1,0:T(...) while((s32[]{:T(128)}, f32[16,128]{1,0:T(8,128)S(1)}, ...), condition=%wide.region_7.9_spmd, body=%wide.region_5.8_spmd.sunk | while | flops 547620288 | bytes 23648676 | solution.py:53
  181.1 4.7 bitcast_reduce_fusion.2
  189.5 5.5 fusion.46
  211.5 77.9 %while.92 = (s32[]{:T(128)}, f32[16,128]{1,0:T(8,128)S(1)}, s32[]{:T(128)}, s32[16]{0:T(128)S(1)}, s32[16,64]{1,0:T(8,128)S(1)}, /*index=5*/bf16[64,128,128]{2,1...) while((s32[]{:T(128)}, f32[16,128]{1,0:T(8,128)S(1)}, ...), condition=%wide.region_4.6_spmd, body=%wide.region_2.5_spmd.sunk | while | flops 272631232 | bytes 6854667 | solution.py:38
  290.6 259.5 %while.93 = (s32[]{:T(128)}, f32[16,128]{1,0:T(8,128)S(1)}, f32[16,128,128]{2,1,0:T(8,128)}, s32[]{:T(128)}, s32[16]{0:T(128)S(1)}, /*index=5*/s32[16,64]{1,0:T(...) while((s32[]{:T(128)}, f32[16,128]{1,0:T(8,128)S(1)}, ...), condition=%wide.region_7.9_spmd, body=%wide.region_5.8_spmd.sunk | while | flops 547620288 | bytes 23648676 | solution.py:53
  301.3 5.5 fusion.46
  317.5 5.5 fusion.46
  333.7 5.5 fusion.46
  349.9 5.5 fusion.46
  366.1 5.5 fusion.46
  382.4 5.5 fusion.46
  398.6 5.5 fusion.46
  414.8 5.5 fusion.46
  431.0 5.5 fusion.46
  447.2 5.5 fusion.46
  463.4 5.5 fusion.46
  479.7 5.5 fusion.46
  495.9 5.5 fusion.46
  512.1 5.5 fusion.46
  528.3 5.5 fusion.46
  544.5 5.5 fusion.46
  553.1 350.7 %all_to_all.75 = bf16[16,128,256]{1,2,0:T(8,128)(2,1)S(1)} all-to-all(bf16[16,128,256]{1,2,0:T(8,128)(2,1)} %bitcast.115), channel_id=1, replica_groups=mesh['clip'=4,'seq'=16,'split'=4] {'seq'}, dimensions={0} | all-to-all | bytes 2097152 | tf_op jit(solution)/shard_map/all_to_all | solution.py:109
  (327 shorter events, 305.1 us)
Async XLA Ops:
  6.5 80.2 %copy-start = (s32[32,64,64]{2,1,0:T(8,128)S(1)}, s32[32,64,64]{2,1,0:T(8,128)}, u32[]{:S(2)}) copy-start(s32[32,64,64]{2,1,0:T(8,128)} %param.18) | copy-start | bytes 1572868
  6.5 87.5 %all-gather.3.cloned.1.call-start = ((), (), s32[]{:S(2)}) async-start(), calls=%async_computation.4 | async-start | bytes 5242880 | tf_op jit(solution)/shard_map/all_gather | solution.py:78
  45.2 101.8 %all-gather.5.cloned.1.call-start = ((), (), s32[]{:S(2)}) async-start(), calls=%async_computation.5 | async-start | bytes 5242880 | tf_op jit(solution)/shard_map/all_gather | solution.py:79
  78.2 1.3 copy-start.1
  79.5 5.8 copy-start.4
  80.9 78.4 %all-to-all-start.1 = ((bf16[128,16,256]{0,2,1:T(8,128)(2,1)}), bf16[128,16,256]{0,2,1:T(8,128)(2,1)}, u32[]{:S(2)}, u32[]{:S(2)}) async-start(bf16[128,16,256]{0,2,1:T(8,128)(2,1)} %bitcast.26), calls=%async_computation.1 | async-start | bytes 2097152 | tf_op jit(solution)/shard_map/all_to_all | solution.py:73
  195.0 2.0 copy-start.2
  197.0 1.0 copy-start.3
  550.1 2.0 copy-start.2
  552.1 1.0 copy-start.3
Sparse Core Ops, SparseCore 0:
  45.4 48.6 all-gather.2
  95.8 51.1 all-gather.4
where the time goes:
time: 919 us; the launch traced here: 912 us
  blocking collectives  418 us (45%)
  matrix products  215 us (23%)
  local copies, waits for them, and re-layouts  188 us (20%)
  waiting for transfers between devices  46.7 us (5%)
  other arithmetic  19.9 us (2%)
  between operations  13.5 us (1%)
    all_to_all x1, blocking collectives, body(): lax.all_to_all(outputs, 'seq', split_axis=0, concat_axis=1, tiled=True)  351 us
    dot_general x34, matrix products, scored(): jnp.einsum('qbd,qjkd->qbjk', q_blocks, k_group, preferred_element_type=jn...  122 us
    dot_general x17, matrix products, accumulate(): jnp.einsum('qbjk,qjkd->qbd', expo.astype(jnp.bfloat16), v_group, preferre...  93.6 us
    gather x34, local copies, waits for them, and re-layouts, scored(): k_group = jnp.take(k_head, picked, axis=0)  72.9 us
    gather x17, local copies, waits for them, and re-layouts, accumulate(): v_group = jnp.take(v_head, picked, axis=0)  62.8 us
    all_gather x1, waiting for transfers between devices, body(): lax.all_gather(v_here, 'split', axis=0, tiled=True)  40.9 us
    all_to_all x1, blocking collectives, body(): lax.all_to_all(k_ready, 'seq', split_axis=1, concat_axis=0, tiled=True)  35.6 us
    all_to_all x1, blocking collectives, body(): lax.all_to_all(v_ready, 'seq', split_axis=1, concat_axis=0, tiled=True)  31.3 us
  transfers between devices with their start and end apart: 3, of which 2 were waited for; matrix products, arithmetic and copies ran while one was open for 3% of the time, Pallas kernels for 0%

commit v1 on v0

v1 whole, which is shorter than its diff:
```python
import functools

import jax
import jax.numpy as jnp
from jax import lax
from jax.experimental import pallas as pl
from jax.experimental.pallas import tpu as pltpu
from jax.sharding import Mesh, PartitionSpec as P

D = 128
BLOCK = 128
GROUP = 4
NEG = -jnp.inf
LOG2E = 1.4426950408889634


def col(ref, head):
    return ref[:, pl.ds(pl.multiple_of(head * D, D), D)]


def prep_kernel(tab, q_ref, k_ref, v_ref, first, second, quer):
    rows, slots = quer.shape[:2]
    near = first.shape[1] // 2
    for r in range(rows):
        for s in range(slots):
            head = tab[r * slots + s]
            ref, i = (first, s) if s < near else (second, s - near)
            ref[r, 2 * i] = col(k_ref, head)
            ref[r, 2 * i + 1] = col(v_ref, head)
            quer[r, s] = col(q_ref, head)


def post_kernel(tab, *refs):
    out = refs[-1]
    slots = sum(x.shape[1] for x in refs[:-1])
    s = 0
    for ref in refs[:-1]:
        for i in range(ref.shape[1]):
            for r in range(ref.shape[0]):
                head = tab[r * slots + s]
                out[:, pl.ds(pl.multiple_of(head * D, D), D)] = ref[r, i]
            s += 1


def dot_t(a, b):
    return lax.dot_general(a, b, (((1,), (1,)), ((), ())), preferred_element_type=jnp.float32)


def dot_n(a, b):
    return lax.dot_general(a, b, (((1,), (0,)), ((), ())), preferred_element_type=jnp.float32)


def soft_step(s, v, state):
    top = jnp.max(s, axis=1, keepdims=True)
    if state is None:
        p = jnp.exp2(s - top)
        return top, jnp.sum(p, axis=1, keepdims=True), dot_n(p.astype(jnp.bfloat16), v)
    m, l, acc = state
    new = jnp.maximum(m, top)
    p = jnp.exp2(s - new)
    fix = jnp.exp2(m - new)
    l = l * fix + jnp.sum(p, axis=1, keepdims=True)
    acc = acc * fix + dot_n(p.astype(jnp.bfloat16), v)
    return new, l, acc


def listed(units, lists, counts, total, factor, q_of, k_of, v_of, put):
    def picked(u, turn):
        spots = []
        for j in range(GROUP):
            slot = turn * GROUP + j
            used = slot < counts[u]
            spots.append((used, lists[u * total + jnp.where(used, slot, 0)]))
        return spots

    def scores(u, spots):
        k = jnp.concatenate([k_of(pos) for _, pos in spots], axis=0)
        s = dot_t(q_of(u), k) * factor
        parts = [jnp.where(used, s[:, j * BLOCK : (j + 1) * BLOCK], NEG) for j, (used, _) in enumerate(spots)]
        return jnp.concatenate(parts, axis=1)

    def vals(spots):
        return jnp.concatenate([v_of(pos) for _, pos in spots], axis=0)

    spots = [picked(u, 0) for u in units]
    s = [scores(u, sp) for u, sp in zip(units, spots)]
    states = [soft_step(x, vals(sp), None) for x, sp in zip(s, spots)]
    for u, state in zip(units, states):
        more = (counts[u] + GROUP - 1) // GROUP

        def step(t, st, u=u):
            sp = picked(u, t)
            return soft_step(scores(u, sp), vals(sp), st)

        _, l, acc = lax.fori_loop(1, more, step, state)
        put(u, (acc / l).astype(jnp.bfloat16))


def attend_head(lists, counts, base, q_of, kv, put):
    members, _, n = kv.shape[:3]
    total = members * n
    factor = D ** -0.5 * LOG2E
    low = counts[base]
    for r in range(1, n):
        low = jnp.minimum(low, counts[base + r])

    @pl.when(low == total)
    def dense():
        wide = n // 2

        def part(i, _):
            q = jnp.concatenate([q_of(i * wide + j) for j in range(wide)], axis=0)
            state = None
            for g in range(members):
                k = kv[g, 0].reshape(n * BLOCK, D)
                v = kv[g, 1].reshape(n * BLOCK, D)
                state = soft_step(dot_t(q, k) * factor, v, state)
            _, l, acc = state
            out = (acc / l).astype(jnp.bfloat16)
            for j in range(wide):
                put(i * wide + j, out[j * BLOCK : (j + 1) * BLOCK])
            return 0

        lax.fori_loop(0, n // wide, part, 0)

    @pl.when(low != total)
    def sparse():
        wide = n // 2

        def part(i, _):
            listed(
                [base + i * wide + j for j in range(wide)], lists, counts, total, factor,
                lambda u: q_of(u - base),
                lambda pos: kv[pos // n, 0, pos % n],
                lambda pos: kv[pos // n, 1, pos % n],
                lambda u, x: put(u - base, x),
            )
            return 0

        lax.fori_loop(0, n // wide, part, 0)


def near_kernel(slot, lists, counts, own, other, q_ref, o_ref, kv, sems):
    half = own.shape[0]
    copies = [
        pltpu.make_async_copy(own, kv.at[pl.ds(0, half)], sems.at[0]),
        pltpu.make_async_copy(other, kv.at[pl.ds(half, half)], sems.at[1]),
    ]
    for copy in copies:
        copy.start()
    for copy in copies:
        copy.wait()

    def put(r, x):
        o_ref[r, 0] = x

    attend_head(lists, counts, 0, lambda r: q_ref[r, slot], kv, put)


def gathered_kernel(skip, lists, counts, q_ref, kv, o_ref):
    n = q_ref.shape[0]
    h = pl.program_id(0)

    def put(r, x):
        o_ref[r, 0] = x

    attend_head(lists, counts, h * n, lambda r: q_ref[r, skip + h], kv.at[:, 0], put)


def local_call(kernel, scalars, inputs, shapes, scratch=(), hbm=0):
    vmem = pl.BlockSpec(memory_space=pltpu.VMEM)
    anywhere = pl.BlockSpec(memory_space=pl.ANY)
    return pl.pallas_call(
        kernel,
        out_shape=[jax.ShapeDtypeStruct(x, jnp.bfloat16) for x in shapes],
        grid_spec=pltpu.PrefetchScalarGridSpec(
            num_scalar_prefetch=len(scalars),
            grid=(),
            in_specs=[anywhere] * hbm + [vmem] * (len(inputs) - hbm),
            out_specs=[vmem] * len(shapes),
            scratch_shapes=list(scratch),
        ),
        compiler_params=pltpu.CompilerParams(vmem_limit_bytes=56 * 2 ** 20),
    )(*scalars, *inputs)


def body(queries, keys, values, key_blocks, block_counts):
    zs = lax.axis_size("z")
    cores = lax.axis_size("core")
    ys = lax.axis_size("split")
    z, c, y = lax.axis_index("z"), lax.axis_index("core"), lax.axis_index("split")
    heads = queries.shape[1] // D
    blocks = key_blocks.shape[1]
    members = cores * ys
    slots = heads // zs

    work = jnp.sum(block_counts, axis=1)
    ids = jnp.arange(heads, dtype=jnp.int32)
    ahead = (work[None, :] > work[:, None]) | ((work[None, :] == work[:, None]) & (ids[None, :] < ids[:, None]))
    rank = jnp.sum(ahead.astype(jnp.int32), axis=1)

    def head_at(places):
        return jnp.sum(jnp.where(rank[None, :] == places[:, None], ids[None, :], 0), axis=1)

    spots = jnp.arange(heads, dtype=jnp.int32)
    row, slot = spots // slots, spots % slots
    table = head_at(slot * zs + jnp.where(slot % 2 == 0, row, zs - 1 - row))
    mine = lax.dynamic_slice_in_dim(table, z * slots, slots)

    q_ids = jnp.arange(zs, dtype=jnp.int32) * members + c * ys + y
    lists = key_blocks[mine[:, None], q_ids[None, :]]
    counts = block_counts[mine[:, None], q_ids[None, :]]
    lz, lc, ly = lists // members, lists // ys % cores, lists % ys
    near = (jnp.arange(slots) == 1)[:, None, None]
    lists = jnp.where(near, (lc + c) % cores * ys + (y - ly) % ys, lc * ys + ly) * zs + lz

    first, second, quer = local_call(
        prep_kernel, [table], [queries, keys, values],
        [(zs, 4, BLOCK, D), (zs, 2 * (slots - 2), BLOCK, D), (zs, slots, BLOCK, D)],
    )

    def swap(x):
        return lax.all_to_all(x, "z", split_axis=0, concat_axis=0, tiled=True)

    def packed(x):
        return x.transpose(1, 0, 2, 3).reshape(-1, D)

    def gathered(x):
        nh = x.shape[0] // (2 * zs * BLOCK)
        x = lax.all_gather(x, ("core", "split"), axis=0, tiled=True)
        return x.reshape(members, nh, 2, zs, BLOCK, D)

    first = swap(first)
    wide_kv, near_kv = packed(first[:, :2]), first[:, 2:].transpose(1, 0, 2, 3)
    wide_kv, near_kv, second = lax.optimization_barrier((wide_kv, near_kv, second))
    wide_kv = gathered(wide_kv)
    near_parts = [near_kv]
    for dy in range(1, ys):
        near_parts.append(lax.ppermute(near_kv, "split", [(i, (i + dy) % ys) for i in range(ys)]))
    second, quer = lax.optimization_barrier((packed(swap(second)), quer))
    light_kv = gathered(second)
    quer, lists, counts = lax.optimization_barrier((swap(quer), lists, counts))

    def attend(slot, kv):
        nh = kv.shape[1]
        return pl.pallas_call(
            functools.partial(gathered_kernel, slot),
            out_shape=jax.ShapeDtypeStruct((zs, nh, BLOCK, D), jnp.bfloat16),
            grid_spec=pltpu.PrefetchScalarGridSpec(
                num_scalar_prefetch=2,
                grid=(nh,),
                in_specs=[
                    pl.BlockSpec(quer.shape, lambda h, *_: (0, 0, 0, 0)),
                    pl.BlockSpec((members, 1, 2, zs, BLOCK, D), lambda h, *_: (0, h, 0, 0, 0, 0)),
                ],
                out_specs=pl.BlockSpec((zs, 1, BLOCK, D), lambda h, *_: (0, h, 0, 0)),
            ),
            compiler_params=pltpu.CompilerParams(vmem_limit_bytes=56 * 2 ** 20),
        )(lists[slot : slot + nh].reshape(-1), counts[slot : slot + nh].reshape(-1), quer, kv)

    wide_out = attend(0, wide_kv)
    near_parts, wide_out = lax.optimization_barrier((near_parts, wide_out))
    near_kv = jnp.stack(near_parts)
    other_kv = lax.ppermute(near_kv, "core", [(0, 1), (1, 0)])
    near_out = local_call(
        functools.partial(near_kernel, 1), [lists[1].reshape(-1), counts[1]],
        [near_kv, other_kv, quer], [(zs, 1, BLOCK, D)],
        [pltpu.VMEM((members, 2, zs, BLOCK, D), jnp.bfloat16), pltpu.SemaphoreType.DMA((2,))],
        hbm=2,
    )[0]
    early_out = swap(wide_out)
    late_out = swap(jnp.concatenate([near_out, attend(2, light_kv)], axis=1))
    return local_call(post_kernel, [table], [early_out, late_out], [queries.shape])[0]


def solution(mesh):
    clips, seqs, splits = mesh.devices.shape
    fine = Mesh(mesh.devices.reshape(clips, seqs // 2, 2, splits), ("clip", "z", "core", "split"))
    tokens = P(("clip", "z", "core", "split"), None)
    return jax.shard_map(
        body,
        mesh=fine,
        in_specs=(tokens, tokens, tokens, P("clip", None, None), P("clip", None)),
        out_specs=tokens,
        check_vma=False,
    )
```

time: 919 us -> 196 us (0.21)
  blocking collectives: 418 us -> 97.1 us
  matrix products: 215 us -> 0 us
  local copies, waits for them, and re-layouts: 188 us -> 8.16 us
  Pallas kernels: 0 us -> 38.3 us
  waiting for transfers between devices: 46.7 us -> 20.5 us
  other arithmetic: 19.9 us -> 4.91 us
    all_to_all x3, blocking collectives: 418 us -> 97.1 us  [swap(): return lax.all_to_all(x, 'z', split_axis=0, concat_axis=0, tiled=True)]
    dot_general x51 -> x0, matrix products: 215 us -> none  [the longest x34 122 us: scored(): jnp.einsum('qbd,qjkd->qbjk', q_blocks, k_group, preferred_element_type=jn...]
    gather x55 -> x3, local copies, waits for them, and re-layouts: 138 us -> 1.5 us  [the longest x2 0.8 us: body(): counts = block_counts[mine[:, None], q_ids[None, :]]]
    all_gather x2, waiting for transfers between devices: 46.7 us -> 1.64 us  [gathered(): x = lax.all_gather(x, ('core', 'split'), axis=0, tiled=True)]
    pallas_call x0 -> x5, Pallas kernels: none -> 38.3 us  [the longest x2 23.8 us: attend(): pl.pallas_call(functools.partial(gathered_kernel, slot), out_shape=jax.Sh...]
    while x15 -> x0, local copies, waits for them, and re-layouts: 20.4 us -> none  [the longest x3 10.6 us: body(): lax.map(whole_head, (jnp.arange(owned, dtype=jnp.int32), lists_mine, coun...]
    all_to_all x1 -> x2, waiting for transfers between devices: 0.01 us -> 18.8 us  [swap(): return lax.all_to_all(x, 'z', split_axis=0, concat_axis=0, tiled=True)]
    select_n x11 -> x0, other arithmetic: 11.8 us -> none  [the longest x2 7.81 us: whole_head(): v_head = jnp.take(v_four, head_place, axis=2)]
  transfers between devices with their start and end apart: 3 -> 8, of which waited for: 2 -> 2; matrix products, arithmetic and copies ran while one was open for 3% -> 5% of each run, Pallas kernels for 0% -> 16%
where the time goes in v1:
time: 196 us; the launch traced here: 195 us
  blocking collectives  97.1 us (50%)
  Pallas kernels  38.3 us (20%)
  waiting for transfers between devices  20.5 us (10%)
  between operations  13.6 us (7%)
  starting transfers between devices  12.1 us (6%)
  local copies, waits for them, and re-layouts  8.16 us (4%)
  other arithmetic  4.91 us (3%)
    all_to_all x3, blocking collectives, swap(): return lax.all_to_all(x, 'z', split_axis=0, concat_axis=0, tiled=True)  97.1 us
    pallas_call x2, Pallas kernels, attend(): pl.pallas_call(functools.partial(gathered_kernel, slot), out_shape=jax.Sh...  23.8 us
    all_to_all x2, waiting for transfers between devices, swap(): return lax.all_to_all(x, 'z', split_axis=0, concat_axis=0, tiled=True)  18.8 us
    pallas_call x3, Pallas kernels, local_call(): pl.pallas_call(kernel, out_shape=[jax.ShapeDtypeStruct(x, jnp.bfloat16) f...  14.5 us
    all_to_all x2, starting transfers between devices, swap(): return lax.all_to_all(x, 'z', split_axis=0, concat_axis=0, tiled=True)  6.99 us
    ppermute x3, starting transfers between devices, body(): lax.ppermute(near_kv, 'split', [(i, (i + dy) % ys) for i in range(ys)])  5 us
  transfers between devices with their start and end apart: 8, of which 2 were waited for; matrix products, arithmetic and copies ran while one was open for 5% of the time, Pallas kernels for 16%

profile of v1, /device:TPU:12, one launch (start us, length us, event | category | flops | bytes accessed | tf_op | source)
XLA Modules:
  0.0 194.7 jit_solution(11238055201847455186)
XLA Ops:
  6.5 0.9 reduce_sum.27
  7.5 0.2 convert_reduce_fusion
  7.6 0.8 select_reduce_fusion.tab
  8.4 5.0 %shard_map.55 = (bf16[8,4,128,128]{3,2,1,0:T(8,128)(2,1)}, bf16[8,4,128,128]{3,2,1,0:T(8,128)(2,1)}, bf16[8,4,128,128]{3,2,1,0:T(8,128)(2,1)}) custom-call(s32[32]{0:T(128)} %select_reduce_fusion.tab, bf16[128,4096]{1,0:T(8,128)(2,1)} %q_ref.1, bf16[128,4096]{1,0:T(8,128)(2,1)} %k_ref.1, bf16[128,4096]{1,0:T(8,128)(2,1)} %v_ref.1), custom_call_target="tpu_custom_call" | custom-call | tf_op jit(solution)/shard_map/pallas_call | solution.py:173
  13.4 37.2 %all_to_all.25 = bf16[8,4,128,128]{3,2,1,0:T(8,128)(2,1)S(1)} all-to-all(bf16[8,4,128,128]{3,2,1,0:T(8,128)(2,1)} %get-tuple-element.21), channel_id=1, replica_groups=mesh['clip'=4,'z'=8,'core'=2,'split'=4] {'z'}, dimensions={0} | all-to-all | bytes 2097152 | tf_op jit(solution)/shard_map/all_to_all | solution.py:223
  50.6 0.1 fusion.22
  50.7 0.8 copy.17
  51.7 0.3 copy-done.7
  52.0 29.7 %all_to_all.26 = bf16[8,4,128,128]{3,2,1,0:T(8,128)(2,1)S(1)} all-to-all(bf16[8,4,128,128]{3,2,1,0:T(8,128)(2,1)S(1)} %copy-done.7), channel_id=1, replica_groups=mesh['clip'=4,'z'=8,'core'=2,'split'=4] {'z'}, dimensions={0} | all-to-all | bytes 2097152 | tf_op jit(solution)/shard_map/all_to_all | solution.py:223
  81.7 1.1 copy.16
  82.8 3.6 %all-to-all-start.2 = ((bf16[8,4,128,128]{3,2,1,0:T(8,128)(2,1)}), bf16[8,4,128,128]{3,2,1,0:T(8,128)(2,1)S(1)}, u32[]{:S(2)}, u32[]{:S(2)}) async-start(bf16[8,4,128,128]{3,2,1,0:T(8,128)(2,1)} %get-tuple-element.26), calls=%async_computation.2 | async-start | bytes 2097152 | tf_op jit(solution)/shard_map/all_to_all | solution.py:223
  86.7 0.7 gather_fusion
  87.4 1.7 collective-permute-start
  89.0 0.9 collective-permute-start.1
  90.0 2.4 %collective-permute-start.2 = (bf16[2,8,128,128]{3,2,1,0:T(8,128)(2,1)S(1)}, bf16[2,8,128,128]{3,2,1,0:T(8,128)(2,1)}, u32[]{:S(2)}, u32[]{:S(2)}) collective-permute-start(bf16[2,8,128,128]{3,2,1,0:T(8,128)(2,1)S(1)} %bitcast.45), channel_id=1, source_target_pairs={{0,3},{1,0},{2,1},{3,2},{4,7},{5,4},{6,5},{7,6},{8,11},{9,8},{10,9... | collective-permute-start | bytes 1572872 | tf_op jit(solution)/shard_map/ppermute | solution.py:239
  92.5 0.7 gather_fusion.1
  93.3 18.8 %all-to-all-done.2.q_ref = bf16[8,4,128,128]{3,2,1,0:T(8,128)(2,1)S(1)} async-done(((bf16[8,4,128,128]{3,2,1,0:T(8,128)(2,1)}), bf16[8,4,128,128]{3,2,1,0:T(8,128)(2,1)S(1)}, u32[]{:S(2)}, u32[]{:S(2)}) %all-to-all-start.2) | async-done | bytes 1048608 | tf_op jit(solution)/shard_map/all_to_all | solution.py:223
  112.1 0.8 reshape.82.lists
  112.8 0.6 slice_bitcast_fusion
  113.4 17.1 %shard_map.56 = bf16[8,1,128,128]{3,2,1,0:T(8,128)(2,1)} custom-call(s32[512]{0:T(512)} %reshape.82.lists, s32[8]{0:T(128)} %get-tuple-element.42.counts, bf16[8,4,128,128]{3,2,1,0:T(8,128)(2,1)} %copy-done.2, bf16[8,1,2,8,128,128]{5,4,3,2,1,0:T(8,128)(2,1)} %bitcast.39), custom_call_target="tpu_custom_call" | custom-call | tf_op jit(solution)/shard_map/pallas_call | solution.py:246
  130.5 0.8 copy-done.9
  131.3 1.7 pad_maximum_fusion.own
  133.1 3.4 %all-to-all-start.3 = ((bf16[8,1,128,128]{3,2,1,0:T(8,128)(2,1)}), bf16[8,1,128,128]{3,2,1,0:T(8,128)(2,1)S(1)}, u32[]{:S(2)}, u32[]{:S(2)}) async-start(bf16[8,1,128,128]{3,2,1,0:T(8,128)(2,1)} %shard_map.56), calls=%async_computation.3 | async-start | bytes 524288 | tf_op jit(solution)/shard_map/all_to_all | solution.py:223
  136.5 0.7 reshape_squeeze.3.lists
  137.2 0.7 reshape.85.lists
  137.9 0.7 reshape.86.counts
  138.5 6.4 %shard_map.57 = bf16[8,1,128,128]{3,2,1,0:T(8,128)(2,1)} custom-call(s32[512]{0:T(512)} %reshape_squeeze.3.lists, s32[8]{0:T(128)} %get-tuple-element.41.counts, bf16[4,2,8,128,128]{4,3,2,1,0:T(8,128)(2,1)} %copy-done.3, bf16[4,2,8,128,128]{4,3,2,1,0:T(8,128)(2,1)} %collective-permute-done.3.other, bf16[8,4,128,128]{3,2,1,0:T(8,128)(2,1)} %copy-done.2), custom_call_target="tpu_custom_call" | custom-call | tf_op jit(solution)/shard_map/pallas_call | solution.py:173
  144.9 1.6 all-gather.5.cloned.1.call-done
  146.5 6.8 %shard_map.58 = bf16[8,2,128,128]{3,2,1,0:T(8,128)(2,1)} custom-call(s32[1024]{0:T(1024)} %reshape.85.lists, s32[16]{0:T(128)} %reshape.86.counts, bf16[8,4,128,128]{3,2,1,0:T(8,128)(2,1)} %copy-done.2, bf16[8,2,2,8,128,128]{5,4,3,2,1,0:T(8,128)(2,1)} %bitcast.38), custom_call_target="tpu_custom_call" | custom-call | tf_op jit(solution)/shard_map/pallas_call | solution.py:246
  153.3 1.1 pad_maximum_fusion.1
  154.5 30.3 %all_to_all.27.refs_1_ = bf16[8,3,128,128]{3,2,1,0:T(8,128)(2,1)} all-to-all(bf16[8,3,128,128]{3,2,1,0:T(8,128)(2,1)S(1)} %pad_maximum_fusion.1), channel_id=1, replica_groups=mesh['clip'=4,'z'=8,'core'=2,'split'=4] {'z'}, dimensions={0} | all-to-all | bytes 1572864 | tf_op jit(solution)/shard_map/all_to_all | solution.py:223
  184.7 3.1 %shard_map.59 = bf16[128,4096]{1,0:T(8,128)(2,1)} custom-call(s32[32]{0:T(128)} %select_reduce_fusion.tab, bf16[8,1,128,128]{3,2,1,0:T(8,128)(2,1)} %copy-done.6, bf16[8,3,128,128]{3,2,1,0:T(8,128)(2,1)} %all_to_all.27.refs_1_), custom_call_target="tpu_custom_call" | custom-call | tf_op jit(solution)/shard_map/pallas_call | solution.py:173
  (43 shorter events, 0.7 us)
Async XLA Ops:
  6.5 80.1 %copy-start = (s32[32,64,64]{2,1,0:T(8,128)S(1)}, s32[32,64,64]{2,1,0:T(8,128)}, u32[]{:S(2)}) copy-start(s32[32,64,64]{2,1,0:T(8,128)} %param.8) | copy-start | bytes 1572868
  6.5 106.9 %all-gather.3.cloned.1.call-start = ((), (), s32[]{:S(2)}) async-start(), calls=%async_computation.5 | async-start | bytes 4718592 | tf_op jit(solution)/shard_map/all_gather | solution.py:230
  50.6 1.4 copy-start.7
  51.6 38.4 %copy-start.4 = (bf16[8,2,128,128]{3,2,0,1:T(8,128)(2,1)}, bf16[8,2,128,128]{3,2,0,1:T(8,128)(2,1)S(1)}, u32[]{:S(2)}) copy-start(bf16[8,2,128,128]{3,2,0,1:T(8,128)(2,1)S(1)} %copy.20) | copy-start | bytes 1572868
  51.7 94.9 %all-gather.5.cloned.1.call-start = ((), (), s32[]{:S(2)}) async-start(), calls=%async_computation.6 | async-start | bytes 9437184 | tf_op jit(solution)/shard_map/all_gather | solution.py:230
  82.8 3.6 %copy-start.10 = (s32[32]{0:T(128)S(1)}, s32[32]{0:T(128)}, u32[]{:S(2)}) copy-start(s32[32]{0:T(128)} %select_reduce_fusion.tab) | copy-start | bytes 388
  82.8 9.7 %copy-start.1 = (s32[32,64]{1,0:T(8,128)S(1)}, s32[32,64]{1,0:T(8,128)}, u32[]{:S(2)}) copy-start(s32[32,64]{1,0:T(8,128)} %param.9) | copy-start | bytes 24580
  82.8 29.2 %all-to-all-start.2 = ((bf16[8,4,128,128]{3,2,1,0:T(8,128)(2,1)}), bf16[8,4,128,128]{3,2,1,0:T(8,128)(2,1)S(1)}, u32[]{:S(2)}, u32[]{:S(2)}) async-start(bf16[8,4,128,128]{3,2,1,0:T(8,128)(2,1)} %get-tuple-element.26), calls=%async_computation.2 | async-start | bytes 2097152 | tf_op jit(solution)/shard_map/all_to_all | solution.py:223
  87.4 43.1 %collective-permute-start = (bf16[2,8,128,128]{3,2,1,0:T(8,128)(2,1)S(1)}, bf16[2,8,128,128]{3,2,1,0:T(8,128)(2,1)}, u32[]{:S(2)}, u32[]{:S(2)}) collective-permute-start(bf16[2,8,128,128]{3,2,1,0:T(8,128)(2,1)S(1)} %bitcast.43), channel_id=1, source_target_pairs={{0,1},{1,2},{2,3},{3,0},{4,5},{5,6},{6,7},{7,4},{8,9},{9,10},{10,1... | collective-permute-start | bytes 1572872 | tf_op jit(solution)/shard_map/ppermute | solution.py:239
  89.0 41.4 %collective-permute-start.1 = (bf16[2,8,128,128]{3,2,1,0:T(8,128)(2,1)S(1)}, bf16[2,8,128,128]{3,2,1,0:T(8,128)(2,1)S(1)}, u32[]{:S(2)}, u32[]{:S(2)}) collective-permute-start(bf16[2,8,128,128]{3,2,1,0:T(8,128)(2,1)S(1)} %bitcast.44), channel_id=1, source_target_pairs={{0,2},{1,3},{2,0},{3,1},{4,6},{5,7},{6,4},{7,5},{8,10},{9,11},{10,... | collective-permute-start | bytes 1572872 | tf_op jit(solution)/shard_map/ppermute | solution.py:239
  90.0 40.5 %collective-permute-start.2 = (bf16[2,8,128,128]{3,2,1,0:T(8,128)(2,1)S(1)}, bf16[2,8,128,128]{3,2,1,0:T(8,128)(2,1)}, u32[]{:S(2)}, u32[]{:S(2)}) collective-permute-start(bf16[2,8,128,128]{3,2,1,0:T(8,128)(2,1)S(1)} %bitcast.45), channel_id=1, source_target_pairs={{0,3},{1,0},{2,1},{3,2},{4,7},{5,4},{6,5},{7,6},{8,11},{9,8},{10,9... | collective-permute-start | bytes 1572872 | tf_op jit(solution)/shard_map/ppermute | solution.py:239
  112.1 1.4 copy-start.2
  113.4 17.9 %copy-start.5 = (bf16[8,2,128,128]{3,2,0,1:T(8,128)(2,1)S(1)}, bf16[8,2,128,128]{3,2,0,1:T(8,128)(2,1)}, u32[]{:S(2)}) copy-start(bf16[8,2,128,128]{3,2,0,1:T(8,128)(2,1)} %copy-done.4) | copy-start | bytes 1572868
  130.5 0.8 copy-start.9
  133.0 5.5 %copy-start.3 = (bf16[4,2,8,128,128]{4,3,2,1,0:T(8,128)(2,1)}, bf16[4,2,8,128,128]{4,3,2,1,0:T(8,128)(2,1)S(1)}, u32[]{:S(2)}) copy-start(bf16[4,2,8,128,128]{4,3,2,1,0:T(8,128)(2,1)S(1)} %pad_maximum_fusion.own) | copy-start | bytes 6291460
  133.0 5.5 %collective-permute-start.3 = (bf16[4,2,8,128,128]{4,3,2,1,0:T(8,128)(2,1)S(1)}, bf16[4,2,8,128,128]{4,3,2,1,0:T(8,128)(2,1)}, u32[]{:S(2)}, u32[]{:S(2)}) collective-permute-start(bf16[4,2,8,128,128]{4,3,2,1,0:T(8,128)(2,1)S(1)} %pad_maximum_fusion.own), channel_id=1, source_target_pairs={{0,4},{4,0},{1,5},{5,1},{2,6},{6,2},{3,7},{7,3},{8,12},{12,8},{9,1... | collective-permute-start | bytes 6291464 | tf_op jit(solution)/shard_map/ppermute | solution.py:264
  133.1 21.4 %all-to-all-start.3 = ((bf16[8,1,128,128]{3,2,1,0:T(8,128)(2,1)}), bf16[8,1,128,128]{3,2,1,0:T(8,128)(2,1)S(1)}, u32[]{:S(2)}, u32[]{:S(2)}) async-start(bf16[8,1,128,128]{3,2,1,0:T(8,128)(2,1)} %shard_map.56), calls=%async_computation.3 | async-start | bytes 524288 | tf_op jit(solution)/shard_map/all_to_all | solution.py:223
  146.5 6.8 %copy-start.8 = (bf16[8,1,128,128]{3,2,1,0:T(8,128)(2,1)S(1)}, bf16[8,1,128,128]{3,2,1,0:T(8,128)(2,1)}, u32[]{:S(2)}) copy-start(bf16[8,1,128,128]{3,2,1,0:T(8,128)(2,1)} %shard_map.57) | copy-start | bytes 786436
  154.5 30.3 %copy-start.6 = (bf16[8,1,128,128]{3,2,1,0:T(8,128)(2,1)}, bf16[8,1,128,128]{3,2,1,0:T(8,128)(2,1)S(1)}, u32[]{:S(2)}) copy-start(bf16[8,1,128,128]{3,2,1,0:T(8,128)(2,1)S(1)} %all-to-all-done.3.refs_0_) | copy-start | bytes 786436
Sparse Core Ops, SparseCore 0:
  51.8 29.8 all-gather.2
  83.5 62.9 all-gather.4

commit v2 on v1

v2 whole, which is shorter than its diff:
```python
import functools

import jax
import jax.numpy as jnp
from jax import lax
from jax.experimental import pallas as pl
from jax.experimental.pallas import tpu as pltpu
from jax.sharding import Mesh, PartitionSpec as P

D = 128
BLOCK = 128
GROUP = 4
NEG = -jnp.inf
LOG2E = 1.4426950408889634


def col(ref, head):
    return ref[:, pl.ds(pl.multiple_of(head * D, D), D)]


def wide_prep(tab, q_ref, k_ref, v_ref, wide):
    for r in range(wide.shape[0]):
        for i, ref in enumerate((q_ref, k_ref, v_ref)):
            wide[r, i] = col(ref, tab[r])


def light_prep(rows, tab, q_ref, k_ref, v_ref, light):
    columns = light.shape[0] // rows
    used = tab.shape[0] // rows - 1
    for r in range(rows):
        for y in range(used):
            head = tab[rows + r * used + y]
            for i, ref in enumerate((q_ref, k_ref, v_ref)):
                light[r * columns + y, i] = col(ref, head)


def post_kernel(rows, tab, light, out):
    columns = light.shape[0] // rows
    used = tab.shape[0] // rows - 1
    for r in range(rows):
        out[:, pl.ds(pl.multiple_of(tab[r] * D, D), D)] = light[r * columns + used]
        for y in range(used):
            at = pl.ds(pl.multiple_of(tab[rows + r * used + y] * D, D), D)
            out[:, at] = light[r * columns + y]


def dot_t(a, b):
    return lax.dot_general(a, b, (((1,), (1,)), ((), ())), preferred_element_type=jnp.float32)


def dot_n(a, b):
    return lax.dot_general(a, b, (((1,), (0,)), ((), ())), preferred_element_type=jnp.float32)


def soft_step(s, v, state):
    top = jnp.max(s, axis=1, keepdims=True)
    if state is None:
        p = jnp.exp2(s - top)
        return top, jnp.sum(p, axis=1, keepdims=True), dot_n(p.astype(jnp.bfloat16), v)
    m, l, acc = state
    new = jnp.maximum(m, top)
    p = jnp.exp2(s - new)
    fix = jnp.exp2(m - new)
    l = l * fix + jnp.sum(p, axis=1, keepdims=True)
    acc = acc * fix + dot_n(p.astype(jnp.bfloat16), v)
    return new, l, acc


def listed(units, lists, counts, total, factor, q_of, k_of, v_of, put):
    def picked(u, turn):
        spots = []
        for j in range(GROUP):
            slot = turn * GROUP + j
            used = slot < counts[u]
            spots.append((used, lists[u * total + jnp.where(used, slot, 0)]))
        return spots

    def scores(u, spots):
        k = jnp.concatenate([k_of(pos) for _, pos in spots], axis=0)
        s = dot_t(q_of(u), k) * factor
        parts = [jnp.where(used, s[:, j * BLOCK : (j + 1) * BLOCK], NEG) for j, (used, _) in enumerate(spots)]
        return jnp.concatenate(parts, axis=1)

    def vals(spots):
        return jnp.concatenate([v_of(pos) for _, pos in spots], axis=0)

    spots = [picked(u, 0) for u in units]
    s = [scores(u, sp) for u, sp in zip(units, spots)]
    states = [soft_step(x, vals(sp), None) for x, sp in zip(s, spots)]
    for u, state in zip(units, states):
        more = (counts[u] + GROUP - 1) // GROUP

        def step(t, st, u=u):
            sp = picked(u, t)
            return soft_step(scores(u, sp), vals(sp), st)

        _, l, acc = lax.fori_loop(1, more, step, state)
        put(u, (acc / l).astype(jnp.bfloat16))


def attend_head(lists, counts, base, q_of, kv, put):
    members, _, n = kv.shape[:3]
    total = members * n
    factor = D ** -0.5 * LOG2E
    low = counts[base]
    for r in range(1, n):
        low = jnp.minimum(low, counts[base + r])

    @pl.when(low == total)
    def dense():
        wide = n // 2

        def part(i, _):
            q = jnp.concatenate([q_of(i * wide + j) for j in range(wide)], axis=0)
            state = None
            for g in range(members):
                k = kv[g, 0].reshape(n * BLOCK, D)
                v = kv[g, 1].reshape(n * BLOCK, D)
                state = soft_step(dot_t(q, k) * factor, v, state)
            _, l, acc = state
            out = (acc / l).astype(jnp.bfloat16)
            for j in range(wide):
                put(i * wide + j, out[j * BLOCK : (j + 1) * BLOCK])
            return 0

        lax.fori_loop(0, n // wide, part, 0)

    @pl.when(low != total)
    def sparse():
        wide = n // 2

        def part(i, _):
            listed(
                [base + i * wide + j for j in range(wide)], lists, counts, total, factor,
                lambda u: q_of(u - base),
                lambda pos: kv[pos // n, 0, pos % n],
                lambda pos: kv[pos // n, 1, pos % n],
                lambda u, x: put(u - base, x),
            )
            return 0

        lax.fori_loop(0, n // wide, part, 0)


def wide_kernel(lists, counts, *refs):
    parts, (q_ref, o_ref, kv, sems) = refs[:-4], refs[-4:]
    copies = [pltpu.make_async_copy(part, kv.at[i], sems.at[i]) for i, part in enumerate(parts)]
    for copy in copies:
        copy.start()
    for copy in copies:
        copy.wait()

    def put(r, x):
        o_ref[r] = x

    attend_head(lists, counts, 0, lambda r: q_ref[r], kv, put)


def hand_on_kernel(counts, *refs):
    passed, (_, out, sems) = refs[:-3], refs[-3:]

    @pl.when(counts[0] == 0)
    def place():
        copies = [pltpu.make_async_copy(ref, out.at[:, y], sems.at[y]) for y, ref in enumerate(passed)]
        for copy in copies:
            copy.start()
        for copy in copies:
            copy.wait()


def light_kernel(total, lists, counts, own, other, o_ref, q_ref, kv, sems):
    units = q_ref.shape[0]

    @pl.when(counts[0] > 0)
    def work():
        copies = [
            pltpu.make_async_copy(own.at[:, 0], q_ref, sems.at[0]),
            pltpu.make_async_copy(own.at[:, 1:], kv.at[pl.ds(0, units)], sems.at[1]),
            pltpu.make_async_copy(other.at[:, 1:], kv.at[pl.ds(units, units)], sems.at[2]),
        ]
        for copy in copies:
            copy.start()
        for copy in copies:
            copy.wait()

        def put(u, x):
            o_ref[u] = x

        wide = 16

        def some(i, _):
            listed(
                [i * wide + j for j in range(wide)], lists, counts, total, D ** -0.5 * LOG2E,
                lambda u: q_ref[u], lambda pos: kv[pos, 0], lambda pos: kv[pos, 1], put,
            )
            return 0

        lax.fori_loop(0, units // wide, some, 0)


def local_call(kernel, scalars, inputs, shapes, scratch=(), hbm=0):
    vmem = pl.BlockSpec(memory_space=pltpu.VMEM)
    anywhere = pl.BlockSpec(memory_space=pl.ANY)
    return pl.pallas_call(
        kernel,
        out_shape=[jax.ShapeDtypeStruct(x, jnp.bfloat16) for x in shapes],
        grid_spec=pltpu.PrefetchScalarGridSpec(
            num_scalar_prefetch=len(scalars),
            grid=(),
            in_specs=[anywhere] * hbm + [vmem] * (len(inputs) - hbm),
            out_specs=[vmem] * len(shapes),
            scratch_shapes=list(scratch),
        ),
        compiler_params=pltpu.CompilerParams(vmem_limit_bytes=56 * 2 ** 20),
    )(*scalars, *inputs)


def body(queries, keys, values, key_blocks, block_counts):
    zs = lax.axis_size("z")
    cores = lax.axis_size("core")
    ys = lax.axis_size("split")
    z, c, y = lax.axis_index("z"), lax.axis_index("core"), lax.axis_index("split")
    heads = queries.shape[1] // D
    blocks = key_blocks.shape[1]
    members = cores * ys

    work = jnp.sum(block_counts, axis=1)
    ids = jnp.arange(heads, dtype=jnp.int32)
    ahead = (work[None, :] > work[:, None]) | ((work[None, :] == work[:, None]) & (ids[None, :] < ids[:, None]))
    rank = jnp.sum(ahead.astype(jnp.int32), axis=1)

    def head_at(places):
        return jnp.sum(jnp.where(rank[None, :] == places[:, None], ids[None, :], 0), axis=1)

    used = heads // zs - 1
    rows = jnp.arange(zs, dtype=jnp.int32)
    columns = jnp.arange(used, dtype=jnp.int32)
    table = head_at(jnp.concatenate([rows, ((1 + columns)[None, :] * zs + rows[:, None]).reshape(-1)]))

    def places(lists):
        return lists // members, lists // ys % cores, lists % ys

    wide_head = lax.dynamic_index_in_dim(table, z, keepdims=False)
    wide_ids = rows * members + c * ys + y
    wide_counts = block_counts[wide_head][wide_ids]
    lz, lc, ly = places(key_blocks[wide_head][wide_ids])
    wide_lists = ((lc + c) % cores * ys + (y - ly) % ys) * zs + lz
    light_head = lax.dynamic_index_in_dim(table, zs + z * used + jnp.minimum(y, used - 1), keepdims=False)
    light_ids = jnp.arange(zs * ys, dtype=jnp.int32)
    light_ids = light_ids // ys * members + c * ys + light_ids % ys
    light_counts = jnp.where(y < used, block_counts[light_head][light_ids], 0)
    lz, lc, ly = places(key_blocks[light_head][light_ids])
    light_lists = (lc + c) % cores * (zs * ys) + lz * ys + ly

    wide = local_call(wide_prep, [table], [queries, keys, values], [(zs, 3, BLOCK, D)])[0]
    light = local_call(
        functools.partial(light_prep, zs), [table], [queries, keys, values], [(zs * ys, 3, BLOCK, D)]
    )[0]

    def spread(x):
        return lax.all_to_all(x, ("z", "split"), split_axis=0, concat_axis=0, tiled=True)

    def over_cores(x):
        return lax.ppermute(x, "core", [(0, 1), (1, 0)])

    wide = lax.all_to_all(wide, "z", split_axis=0, concat_axis=0, tiled=True)
    wide, wide_lists, wide_counts, light_lists, light_counts = lax.optimization_barrier(
        (wide, wide_lists, wide_counts, light_lists, light_counts)
    )
    wide_q, wide_kv = wide[:, 0], wide[:, 1:].transpose(1, 0, 2, 3)
    wide_q, wide_kv, light = lax.optimization_barrier((wide_q, wide_kv, light))
    parts = [wide_kv]
    for dy in range(1, ys):
        parts.append(lax.ppermute(wide_kv, "split", [(i, (i + dy) % ys) for i in range(ys)]))
    parts = parts + [over_cores(x) for x in parts]
    light = spread(light)
    wide_out = local_call(
        wide_kernel, [wide_lists.reshape(-1), wide_counts], [*parts, wide_q], [(zs, BLOCK, D)],
        [pltpu.VMEM((members, 2, zs, BLOCK, D), jnp.bfloat16), pltpu.SemaphoreType.DMA((members,))],
        hbm=members,
    )[0]
    light, wide_out = lax.optimization_barrier((light, wide_out))
    light_out = local_call(
        functools.partial(light_kernel, blocks), [light_lists.reshape(-1), light_counts],
        [light, over_cores(light)], [(zs * ys, BLOCK, D)],
        [
            pltpu.VMEM((zs * ys, BLOCK, D), jnp.bfloat16),
            pltpu.VMEM((blocks, 2, BLOCK, D), jnp.bfloat16),
            pltpu.SemaphoreType.DMA((3,)),
        ],
        hbm=2,
    )[0]
    passed = [lax.ppermute(wide_out, "split", [(i, used)]) for i in range(used)] + [wide_out]
    anywhere = pl.BlockSpec(memory_space=pl.ANY)
    light_out = pl.pallas_call(
        hand_on_kernel,
        out_shape=jax.ShapeDtypeStruct((zs, ys, BLOCK, D), jnp.bfloat16),
        grid_spec=pltpu.PrefetchScalarGridSpec(
            num_scalar_prefetch=1,
            grid=(),
            in_specs=[pl.BlockSpec(memory_space=pltpu.VMEM)] * ys + [anywhere],
            out_specs=anywhere,
            scratch_shapes=[pltpu.SemaphoreType.DMA((ys,))],
        ),
        input_output_aliases={ys + 1: 0},
    )(light_counts, *passed, light_out.reshape(zs, ys, BLOCK, D))
    light_out = spread(light_out.reshape(zs * ys, BLOCK, D))
    return local_call(functools.partial(post_kernel, zs), [table], [light_out], [queries.shape])[0]


def solution(mesh):
    clips, seqs, splits = mesh.devices.shape
    fine = Mesh(mesh.devices.reshape(clips, seqs // 2, 2, splits), ("clip", "z", "core", "split"))
    tokens = P(("clip", "z", "core", "split"), None)
    return jax.shard_map(
        body,
        mesh=fine,
        in_specs=(tokens, tokens, tokens, P("clip", None, None), P("clip", None)),
        out_specs=tokens,
        check_vma=False,
    )
```

time: 196 us -> 182 us (0.929)
  blocking collectives: 97.1 us -> 42.7 us
  waiting for transfers between devices: 20.5 us -> 57.1 us
  starting transfers between devices: 12.1 us -> 27.2 us
  between operations: 13.6 us -> 3.91 us
  other arithmetic: 4.91 us -> 2.47 us
    all_to_all x3 -> x1, blocking collectives: 97.1 us -> 42.7 us  [spread(): lax.all_to_all(x, ('z', 'split'), split_axis=0, concat_axis=0, tiled=True)]
    ppermute x4 -> x11, waiting for transfers between devices: 0.01 us -> 46.3 us  [the longest x3 44.7 us: body(): lax.ppermute(wide_kv, 'split', [(i, (i + dy) % ys) for i in range(ys)])]
    pallas_call x3 -> x5, Pallas kernels: 14.5 us -> 37.5 us  [local_call(): pl.pallas_call(kernel, out_shape=[jax.ShapeDtypeStruct(x, jnp.bfloat16) f...]
    pallas_call x2 -> x1, Pallas kernels: 23.8 us -> 1.88 us  [body(): pl.pallas_call(hand_on_kernel, out_shape=jax.ShapeDtypeStruct((zs, ys, BL...]
    ppermute x4 -> x11, starting transfers between devices: 5.1 us -> 13.6 us  [the longest x3 8.34 us: body(): lax.ppermute(wide_out, 'split', [(i, used)])]
    all_to_all x2, waiting for transfers between devices: 18.8 us -> 10.7 us  [the longest x1 8.79 us: body(): wide = lax.all_to_all(wide, 'z', split_axis=0, concat_axis=0, tiled=True)]
    all_to_all x2, starting transfers between devices: 6.99 us -> 13.5 us  [the longest x1 8.47 us: body(): wide = lax.all_to_all(wide, 'z', split_axis=0, concat_axis=0, tiled=True)]
  transfers between devices with their start and end apart: 8 -> 13, of which waited for: 2 -> 5; matrix products, arithmetic and copies ran while one was open for 5% -> 4% of each run, Pallas kernels for 16% -> 17%
where the time goes in v2:
time: 182 us
  waiting for transfers between devices  57.1 us (31%)
  blocking collectives  42.7 us (23%)
  Pallas kernels  39.4 us (22%)
  starting transfers between devices  27.2 us (15%)
  local copies, waits for them, and re-layouts  8.81 us (5%)
  between operations  3.91 us (2%)
  other arithmetic  2.47 us (1%)
    ppermute x3, waiting for transfers between devices, body(): lax.ppermute(wide_kv, 'split', [(i, (i + dy) % ys) for i in range(ys)])  44.7 us
    all_to_all x1, blocking collectives, spread(): lax.all_to_all(x, ('z', 'split'), split_axis=0, concat_axis=0, tiled=True)  42.7 us
    pallas_call x5, Pallas kernels, local_call(): pl.pallas_call(kernel, out_shape=[jax.ShapeDtypeStruct(x, jnp.bfloat16) f...  37.5 us
    all_to_all x1, waiting for transfers between devices, body(): wide = lax.all_to_all(wide, 'z', split_axis=0, concat_axis=0, tiled=True)  8.79 us
    all_to_all x1, starting transfers between devices, body(): wide = lax.all_to_all(wide, 'z', split_axis=0, concat_axis=0, tiled=True)  8.47 us
    ppermute x3, starting transfers between devices, body(): lax.ppermute(wide_out, 'split', [(i, used)])  8.34 us
    all_to_all x1, starting transfers between devices, spread(): lax.all_to_all(x, ('z', 'split'), split_axis=0, concat_axis=0, tiled=True)  5.07 us
    ppermute x3, starting transfers between devices, body(): lax.ppermute(wide_kv, 'split', [(i, (i + dy) % ys) for i in range(ys)])  4.78 us
  transfers between devices with their start and end apart: 13, of which 5 were waited for; matrix products, arithmetic and copies ran while one was open for 4% of the time, Pallas kernels for 17%

profile of v2, /device:TPU:12, one launch (start us, length us, event | category | flops | bytes accessed | tf_op | source)
XLA Modules:
  0.0 181.6 jit_solution(16595113548659939586)
XLA Ops:
  0.1 0.8 reduce_sum.27
  1.2 0.8 select_reduce_fusion.tab
  2.0 3.7 %shard_map.55 = bf16[8,3,128,128]{3,2,1,0:T(8,128)(2,1)} custom-call(s32[32]{0:T(128)} %select_reduce_fusion.tab, bf16[128,4096]{1,0:T(8,128)(2,1)} %q_ref.3, bf16[128,4096]{1,0:T(8,128)(2,1)} %k_ref.3, bf16[128,4096]{1,0:T(8,128)(2,1)} %v_ref.3), custom_call_target="tpu_custom_call" | custom-call | tf_op jit(solution)/shard_map/pallas_call | solution.py:204
  5.7 8.5 %all-to-all-start = ((bf16[8,3,128,128]{3,2,1,0:T(8,128)(2,1)}), bf16[8,3,128,128]{3,2,1,0:T(8,128)(2,1)S(1)}, u32[]{:S(2)}, u32[]{:S(2)}) async-start(bf16[8,3,128,128]{3,2,1,0:T(8,128)(2,1)} %shard_map.55), calls=%async_computation | async-start | bytes 1572864 | tf_op jit(solution)/shard_map/all_to_all | solution.py:266
  14.2 0.6 fusion.33
  17.3 4.8 %shard_map.56 = bf16[32,3,128,128]{3,2,1,0:T(8,128)(2,1)} custom-call(s32[32]{0:T(128)} %select_reduce_fusion.tab, bf16[128,4096]{1,0:T(8,128)(2,1)} %q_ref.3, bf16[128,4096]{1,0:T(8,128)(2,1)} %k_ref.3, bf16[128,4096]{1,0:T(8,128)(2,1)} %v_ref.3), custom_call_target="tpu_custom_call" | custom-call | tf_op jit(solution)/shard_map/pallas_call | solution.py:204
  23.4 0.8 dynamic-slice_bitcast_fusion
  24.7 0.7 fusion.28
  25.4 0.7 gather_fusion.3
  26.7 1.2 gather_fusion.1
  28.5 8.8 %all-to-all-done = bf16[8,3,128,128]{3,2,1,0:T(8,128)(2,1)S(1)} async-done(((bf16[8,3,128,128]{3,2,1,0:T(8,128)(2,1)}), bf16[8,3,128,128]{3,2,1,0:T(8,128)(2,1)S(1)}, u32[]{:S(2)}, u32[]{:S(2)}) %all-to-all-start) | async-done | bytes 786464 | tf_op jit(solution)/shard_map/all_to_all | solution.py:266
  37.3 0.8 slice_bitcast_fusion.refs_0_
  38.1 0.7 slice_bitcast_fusion.1.refs_8_
  38.8 5.1 %all-to-all-start.1 = ((bf16[32,3,128,128]{3,2,1,0:T(8,128)(2,1)}), bf16[32,3,128,128]{3,2,1,0:T(8,128)(2,1)S(1)}, u32[]{:S(2)}, u32[]{:S(2)}) async-start(bf16[32,3,128,128]{3,2,1,0:T(8,128)(2,1)} %shard_map.56), calls=%async_computation.1 | async-start | bytes 6291456 | tf_op jit(solution)/shard_map/all_to_all | solution.py:261
  43.9 1.5 collective-permute-start
  45.5 0.8 collective-permute-start.1
  46.3 2.4 %collective-permute-start.2 = (bf16[2,8,128,128]{3,2,1,0:T(8,128)(2,1)}, bf16[2,8,128,128]{3,2,1,0:T(8,128)(2,1)}, u32[]{:S(2)}, u32[]{:S(2)}) collective-permute-start(bf16[2,8,128,128]{3,2,1,0:T(8,128)(2,1)} %slice_bitcast_fusion.refs_0_), channel_id=1, source_target_pairs={{0,3},{1,0},{2,1},{3,2},{4,7},{5,4},{6,5},{7,6},{8,11},{9,8},{10,9... | collective-permute-start | bytes 1572872 | tf_op jit(solution)/shard_map/ppermute | solution.py:274
  48.7 30.6 %collective-permute-done.refs_1_ = bf16[2,8,128,128]{3,2,1,0:T(8,128)(2,1)} collective-permute-done((bf16[2,8,128,128]{3,2,1,0:T(8,128)(2,1)}, bf16[2,8,128,128]{3,2,1,0:T(8,128)(2,1)}, u32[]{:S(2)}, u32[]{:S(2)}) %collective-permute-start) | collective-permute-done | bytes 524320 | tf_op jit(solution)/shard_map/ppermute | solution.py:274
  79.8 14.2 %collective-permute-done.2.refs_3_ = bf16[2,8,128,128]{3,2,1,0:T(8,128)(2,1)} collective-permute-done((bf16[2,8,128,128]{3,2,1,0:T(8,128)(2,1)}, bf16[2,8,128,128]{3,2,1,0:T(8,128)(2,1)}, u32[]{:S(2)}, u32[]{:S(2)}) %collective-permute-start.2) | collective-permute-done | bytes 524320 | tf_op jit(solution)/shard_map/ppermute | solution.py:274
  94.0 0.7 reshape.115.lists
  94.6 1.6 collective-permute-done.6.refs_7_
  96.2 17.2 %shard_map.57.refs_3_ = bf16[8,128,128]{2,1,0:T(8,128)(2,1)} custom-call(s32[512]{0:T(512)} %reshape.115.lists, s32[8]{0:T(128)} %gather_fusion.1, bf16[2,8,128,128]{3,2,1,0:T(8,128)(2,1)} %slice_bitcast_fusion.refs_0_, bf16[2,8,128,128]{3,2,1,0:T(8,128)(2,1)} %collective-permute-done.refs_1_, bf16[2,8,128,128]{3,2,1,0:T(8,128)(2,1)} %collective-permute-done.1.refs_2_, ...), custom_call_target="tpu_custom_call" | custom-call | tf_op jit(solution)/shard_map/pallas_call | solution.py:204
  113.5 1.9 %all-to-all-done.1.own = bf16[32,3,128,128]{3,2,1,0:T(8,128)(2,1)S(1)} async-done(((bf16[32,3,128,128]{3,2,1,0:T(8,128)(2,1)}), bf16[32,3,128,128]{3,2,1,0:T(8,128)(2,1)S(1)}, u32[]{:S(2)}, u32[]{:S(2)}) %all-to-all-start.1) | async-done | bytes 3145760 | tf_op jit(solution)/shard_map/all_to_all | solution.py:261
  115.4 0.7 collective-permute-start.7
  116.1 6.3 %collective-permute-start.8 = (bf16[8,128,128]{2,1,0:T(8,128)(2,1)}, bf16[8,128,128]{2,1,0:T(8,128)(2,1)}, u32[]{:S(2)}, u32[]{:S(2)}) collective-permute-start(bf16[8,128,128]{2,1,0:T(8,128)(2,1)} %shard_map.57.refs_3_), channel_id=1, source_target_pairs={{1,3},{5,7},{9,11},{13,15},{17,19},{21,23},{25,27},{29,31},{33,35}... | collective-permute-start | bytes 786440 | tf_op jit(solution)/shard_map/ppermute | solution.py:293
  122.4 1.4 collective-permute-start.9
  123.8 0.7 reshape.116.lists
  124.4 8.6 %shard_map.58 = bf16[32,128,128]{2,1,0:T(8,128)(2,1)} custom-call(s32[2048]{0:T(1024)} %reshape.116.lists, s32[32]{0:T(128)} %broadcast_select_fusion.counts, bf16[32,3,128,128]{3,2,1,0:T(8,128)(2,1)} %copy-done, bf16[32,3,128,128]{3,2,1,0:T(8,128)(2,1)} %collective-permute-done.10.other), custom_call_target="tpu_custom_call" | custom-call | tf_op jit(solution)/shard_map/pallas_call | solution.py:204
  133.1 0.7 copy-done.1
  133.8 1.9 %shard_map.59 = bf16[8,4,128,128]{3,2,1,0:T(8,128)(2,1)} custom-call(s32[32]{0:T(128)} %broadcast_select_fusion.counts, bf16[8,128,128]{2,1,0:T(8,128)(2,1)} %copy-done.1, bf16[8,128,128]{2,1,0:T(8,128)(2,1)} %collective-permute-done.8.refs_1_, bf16[8,128,128]{2,1,0:T(8,128)(2,1)} %collective-permute-done.9.refs_2_, ...), custom_call_target="tpu_custom_call", output_to_operand_aliasing={{}: (5, {})} | custom-call | tf_op jit(solution)/shard_map/pallas_call | solution.py:295
  135.7 42.7 %all_to_all.15.light = bf16[32,128,128]{2,1,0:T(8,128)(2,1)} all-to-all(bf16[32,128,128]{2,1,0:T(8,128)(2,1)} %bitcast.21), channel_id=1, replica_groups=mesh['clip'=4,'z'=8,'core'=2,'split'=4] {'z','split'}, dimensions={0} | all-to-all | bytes 2097152 | tf_op jit(solution)/shard_map/all_to_all | solution.py:261
  178.4 3.1 %shard_map.60 = bf16[128,4096]{1,0:T(8,128)(2,1)} custom-call(s32[32]{0:T(128)} %select_reduce_fusion.tab, bf16[32,128,128]{2,1,0:T(8,128)(2,1)} %all_to_all.15.light), custom_call_target="tpu_custom_call" | custom-call | tf_op jit(solution)/shard_map/pallas_call | solution.py:204
  (33 shorter events, 2.6 us)
Async XLA Ops:
  2.0 12.2 %copy-start.2 = (s32[32]{0:T(128)S(1)}, s32[32]{0:T(128)}, u32[]{:S(2)}) copy-start(s32[32]{0:T(128)} %select_reduce_fusion.tab) | copy-start | bytes 388
  5.7 31.6 %all-to-all-start = ((bf16[8,3,128,128]{3,2,1,0:T(8,128)(2,1)}), bf16[8,3,128,128]{3,2,1,0:T(8,128)(2,1)S(1)}, u32[]{:S(2)}, u32[]{:S(2)}) async-start(bf16[8,3,128,128]{3,2,1,0:T(8,128)(2,1)} %shard_map.55), calls=%async_computation | async-start | bytes 1572864 | tf_op jit(solution)/shard_map/all_to_all | solution.py:266
  38.8 76.6 %all-to-all-start.1 = ((bf16[32,3,128,128]{3,2,1,0:T(8,128)(2,1)}), bf16[32,3,128,128]{3,2,1,0:T(8,128)(2,1)S(1)}, u32[]{:S(2)}, u32[]{:S(2)}) async-start(bf16[32,3,128,128]{3,2,1,0:T(8,128)(2,1)} %shard_map.56), calls=%async_computation.1 | async-start | bytes 6291456 | tf_op jit(solution)/shard_map/all_to_all | solution.py:261
  43.9 35.4 %collective-permute-start = (bf16[2,8,128,128]{3,2,1,0:T(8,128)(2,1)}, bf16[2,8,128,128]{3,2,1,0:T(8,128)(2,1)}, u32[]{:S(2)}, u32[]{:S(2)}) collective-permute-start(bf16[2,8,128,128]{3,2,1,0:T(8,128)(2,1)} %slice_bitcast_fusion.refs_0_), channel_id=1, source_target_pairs={{0,1},{1,2},{2,3},{3,0},{4,5},{5,6},{6,7},{7,4},{8,9},{9,10},{10,1... | collective-permute-start | bytes 1572872 | tf_op jit(solution)/shard_map/ppermute | solution.py:274
  45.5 33.8 %collective-permute-start.1 = (bf16[2,8,128,128]{3,2,1,0:T(8,128)(2,1)}, bf16[2,8,128,128]{3,2,1,0:T(8,128)(2,1)}, u32[]{:S(2)}, u32[]{:S(2)}) collective-permute-start(bf16[2,8,128,128]{3,2,1,0:T(8,128)(2,1)} %slice_bitcast_fusion.refs_0_), channel_id=1, source_target_pairs={{0,2},{1,3},{2,0},{3,1},{4,6},{5,7},{6,4},{7,5},{8,10},{9,11},{10,... | collective-permute-start | bytes 1572872 | tf_op jit(solution)/shard_map/ppermute | solution.py:274
  46.3 47.6 %collective-permute-start.2 = (bf16[2,8,128,128]{3,2,1,0:T(8,128)(2,1)}, bf16[2,8,128,128]{3,2,1,0:T(8,128)(2,1)}, u32[]{:S(2)}, u32[]{:S(2)}) collective-permute-start(bf16[2,8,128,128]{3,2,1,0:T(8,128)(2,1)} %slice_bitcast_fusion.refs_0_), channel_id=1, source_target_pairs={{0,3},{1,0},{2,1},{3,2},{4,7},{5,4},{6,5},{7,6},{8,11},{9,8},{10,9... | collective-permute-start | bytes 1572872 | tf_op jit(solution)/shard_map/ppermute | solution.py:274
  48.7 45.9 %collective-permute-start.3 = (bf16[2,8,128,128]{3,2,1,0:T(8,128)(2,1)}, bf16[2,8,128,128]{3,2,1,0:T(8,128)(2,1)}, u32[]{:S(2)}, u32[]{:S(2)}) collective-permute-start(bf16[2,8,128,128]{3,2,1,0:T(8,128)(2,1)} %slice_bitcast_fusion.refs_0_), channel_id=1, source_target_pairs={{0,4},{4,0},{1,5},{5,1},{2,6},{6,2},{3,7},{7,3},{8,12},{12,8},{9,1... | collective-permute-start | bytes 1572872 | tf_op jit(solution)/shard_map/ppermute | solution.py:264
  79.3 15.3 %collective-permute-start.4 = (bf16[2,8,128,128]{3,2,1,0:T(8,128)(2,1)}, bf16[2,8,128,128]{3,2,1,0:T(8,128)(2,1)}, u32[]{:S(2)}, u32[]{:S(2)}) collective-permute-start(bf16[2,8,128,128]{3,2,1,0:T(8,128)(2,1)} %collective-permute-done.refs_1_), channel_id=1, source_target_pairs={{0,4},{4,0},{1,5},{5,1},{2,6},{6,2},{3,7},{7,3},{8,12},{12,8},{9,1... | collective-permute-start | bytes 1572872 | tf_op jit(solution)/shard_map/ppermute | solution.py:264
  79.3 15.3 %collective-permute-start.5 = (bf16[2,8,128,128]{3,2,1,0:T(8,128)(2,1)}, bf16[2,8,128,128]{3,2,1,0:T(8,128)(2,1)}, u32[]{:S(2)}, u32[]{:S(2)}) collective-permute-start(bf16[2,8,128,128]{3,2,1,0:T(8,128)(2,1)} %collective-permute-done.1.refs_2_), channel_id=1, source_target_pairs={{0,4},{4,0},{1,5},{5,1},{2,6},{6,2},{3,7},{7,3},{8,12},{12,8},{9,1... | collective-permute-start | bytes 1572872 | tf_op jit(solution)/shard_map/ppermute | solution.py:264
  94.0 2.3 %collective-permute-start.6 = (bf16[2,8,128,128]{3,2,1,0:T(8,128)(2,1)}, bf16[2,8,128,128]{3,2,1,0:T(8,128)(2,1)}, u32[]{:S(2)}, u32[]{:S(2)}) collective-permute-start(bf16[2,8,128,128]{3,2,1,0:T(8,128)(2,1)} %collective-permute-done.2.refs_3_), channel_id=1, source_target_pairs={{0,4},{4,0},{1,5},{5,1},{2,6},{6,2},{3,7},{7,3},{8,12},{12,8},{9,1... | collective-permute-start | bytes 1572872 | tf_op jit(solution)/shard_map/ppermute | solution.py:264
  115.4 9.0 %copy-start = (bf16[32,3,128,128]{3,2,1,0:T(8,128)(2,1)}, bf16[32,3,128,128]{3,2,1,0:T(8,128)(2,1)S(1)}, u32[]{:S(2)}) copy-start(bf16[32,3,128,128]{3,2,1,0:T(8,128)(2,1)S(1)} %all-to-all-done.1.own) | copy-start | bytes 9437188
  115.4 9.0 %collective-permute-start.10 = (bf16[32,3,128,128]{3,2,1,0:T(8,128)(2,1)S(1)}, bf16[32,3,128,128]{3,2,1,0:T(8,128)(2,1)}, u32[]{:S(2)}, u32[]{:S(2)}) collective-permute-start(bf16[32,3,128,128]{3,2,1,0:T(8,128)(2,1)S(1)} %all-to-all-done.1.own), channel_id=1, source_target_pairs={{0,4},{4,0},{1,5},{5,1},{2,6},{6,2},{3,7},{7,3},{8,12},{12,8},{9,1... | collective-permute-start | bytes 9437192 | tf_op jit(solution)/shard_map/ppermute | solution.py:264
  115.4 17.7 %collective-permute-start.7 = (bf16[8,128,128]{2,1,0:T(8,128)(2,1)}, bf16[8,128,128]{2,1,0:T(8,128)(2,1)S(1)}, u32[]{:S(2)}, u32[]{:S(2)}) collective-permute-start(bf16[8,128,128]{2,1,0:T(8,128)(2,1)} %shard_map.57.refs_3_), channel_id=1, source_target_pairs={{0,3},{4,7},{8,11},{12,15},{16,19},{20,23},{24,27},{28,31},{32,35}... | collective-permute-start | bytes 786440 | tf_op jit(solution)/shard_map/ppermute | solution.py:293
  116.1 17.0 %collective-permute-start.8 = (bf16[8,128,128]{2,1,0:T(8,128)(2,1)}, bf16[8,128,128]{2,1,0:T(8,128)(2,1)}, u32[]{:S(2)}, u32[]{:S(2)}) collective-permute-start(bf16[8,128,128]{2,1,0:T(8,128)(2,1)} %shard_map.57.refs_3_), channel_id=1, source_target_pairs={{1,3},{5,7},{9,11},{13,15},{17,19},{21,23},{25,27},{29,31},{33,35}... | collective-permute-start | bytes 786440 | tf_op jit(solution)/shard_map/ppermute | solution.py:293
  122.4 10.7 %collective-permute-start.9 = (bf16[8,128,128]{2,1,0:T(8,128)(2,1)}, bf16[8,128,128]{2,1,0:T(8,128)(2,1)}, u32[]{:S(2)}, u32[]{:S(2)}) collective-permute-start(bf16[8,128,128]{2,1,0:T(8,128)(2,1)} %shard_map.57.refs_3_), channel_id=1, source_target_pairs={{2,3},{6,7},{10,11},{14,15},{18,19},{22,23},{26,27},{30,31},{34,35... | collective-permute-start | bytes 786440 | tf_op jit(solution)/shard_map/ppermute | solution.py:293
  133.1 0.7 copy-start.1

commit v3 on v2

--- a/solution.py
+++ b/solution.py
@@ -18,10 +18,16 @@
     return ref[:, pl.ds(pl.multiple_of(head * D, D), D)]
 
 
-def wide_prep(tab, q_ref, k_ref, v_ref, wide):
+def wide_prep(tab, q_ref, k_ref, v_ref, wide, sems):
+    copies = []
     for r in range(wide.shape[0]):
+        at = pl.ds(pl.multiple_of(tab[r] * D, D), D)
         for i, ref in enumerate((q_ref, k_ref, v_ref)):
-            wide[r, i] = col(ref, tab[r])
+            copies.append(pltpu.make_async_copy(ref.at[:, at], wide.at[r, i], sems.at[r, i]))
+    for copy in copies:
+        copy.start()
+    for copy in copies:
+        copy.wait()
 
 
 def light_prep(rows, tab, q_ref, k_ref, v_ref, light):
@@ -142,9 +148,13 @@
         lax.fori_loop(0, n // wide, part, 0)
 
 
-def wide_kernel(lists, counts, *refs):
-    parts, (q_ref, o_ref, kv, sems) = refs[:-4], refs[-4:]
-    copies = [pltpu.make_async_copy(part, kv.at[i], sems.at[i]) for i, part in enumerate(parts)]
+def wide_kernel(lists, counts, q_hbm, *refs):
+    parts, (o_ref, q_ref, kv, sems) = refs[:-4], refs[-4:]
+    spots = []
+    for at in (0, kv.shape[0] // 2):
+        spots += [kv.at[at], kv.at[at + 1], kv.at[at + 3], kv.at[at + 2, 0], kv.at[at + 2, 1]]
+    copies = [pltpu.make_async_copy(part, spot, sems.at[i]) for i, (part, spot) in enumerate(zip(parts, spots))]
+    copies.append(pltpu.make_async_copy(q_hbm.at[:, 0], q_ref, sems.at[len(parts)]))
     for copy in copies:
         copy.start()
     for copy in copies:
@@ -157,7 +167,7 @@
 
 
 def hand_on_kernel(counts, *refs):
-    passed, (_, out, sems) = refs[:-3], refs[-3:]
+    passed, (light, out, sems) = refs[:-3], refs[-3:]
 
     @pl.when(counts[0] == 0)
     def place():
@@ -166,6 +176,10 @@
             copy.start()
         for copy in copies:
             copy.wait()
+
+    @pl.when(counts[0] > 0)
+    def keep():
+        out[...] = light[...]
 
 
 def light_kernel(total, lists, counts, own, other, o_ref, q_ref, kv, sems):
@@ -252,7 +266,9 @@
     lz, lc, ly = places(key_blocks[light_head][light_ids])
     light_lists = (lc + c) % cores * (zs * ys) + lz * ys + ly
 
-    wide = local_call(wide_prep, [table], [queries, keys, values], [(zs, 3, BLOCK, D)])[0]
+    wide = local_call(
+        wide_prep, [table], [queries, keys, values], [(zs, 3, BLOCK, D)], [pltpu.SemaphoreType.DMA((zs, 3))], hbm=3
+    )[0]
     light = local_call(
         functools.partial(light_prep, zs), [table], [queries, keys, values], [(zs * ys, 3, BLOCK, D)]
     )[0]
@@ -264,20 +280,26 @@
         return lax.ppermute(x, "core", [(0, 1), (1, 0)])
 
     wide = lax.all_to_all(wide, "z", split_axis=0, concat_axis=0, tiled=True)
-    wide, wide_lists, wide_counts, light_lists, light_counts = lax.optimization_barrier(
-        (wide, wide_lists, wide_counts, light_lists, light_counts)
+    wide, light, wide_lists, wide_counts, light_lists, light_counts = lax.optimization_barrier(
+        (wide, light, wide_lists, wide_counts, light_lists, light_counts)
     )
-    wide_q, wide_kv = wide[:, 0], wide[:, 1:].transpose(1, 0, 2, 3)
-    wide_q, wide_kv, light = lax.optimization_barrier((wide_q, wide_kv, light))
-    parts = [wide_kv]
-    for dy in range(1, ys):
-        parts.append(lax.ppermute(wide_kv, "split", [(i, (i + dy) % ys) for i in range(ys)]))
+    wide_kv = wide[:, 1:].transpose(1, 0, 2, 3)
+
+    def over_y(x, dy):
+        return lax.ppermute(x, "split", [(i, (i + dy) % ys) for i in range(ys)])
+
+    before, after = over_y(wide_kv, 1), over_y(wide_kv, -1)
+    parts = [wide_kv, before, after, over_y(before[0], 1), over_y(after[1], -1)]
     parts = parts + [over_cores(x) for x in parts]
     light = spread(light)
     wide_out = local_call(
-        wide_kernel, [wide_lists.reshape(-1), wide_counts], [*parts, wide_q], [(zs, BLOCK, D)],
-        [pltpu.VMEM((members, 2, zs, BLOCK, D), jnp.bfloat16), pltpu.SemaphoreType.DMA((members,))],
-        hbm=members,
+        wide_kernel, [wide_lists.reshape(-1), wide_counts], [wide, *parts], [(zs, BLOCK, D)],
+        [
+            pltpu.VMEM((zs, BLOCK, D), jnp.bfloat16),
+            pltpu.VMEM((members, 2, zs, BLOCK, D), jnp.bfloat16),
+            pltpu.SemaphoreType.DMA((len(parts) + 1,)),
+        ],
+        hbm=len(parts) + 1,
     )[0]
     light, wide_out = lax.optimization_barrier((light, wide_out))
     light_out = local_call(
@@ -291,19 +313,10 @@
         hbm=2,
     )[0]
     passed = [lax.ppermute(wide_out, "split", [(i, used)]) for i in range(used)] + [wide_out]
-    anywhere = pl.BlockSpec(memory_space=pl.ANY)
-    light_out = pl.pallas_call(
-        hand_on_kernel,
-        out_shape=jax.ShapeDtypeStruct((zs, ys, BLOCK, D), jnp.bfloat16),
-        grid_spec=pltpu.PrefetchScalarGridSpec(
-            num_scalar_prefetch=1,
-            grid=(),
-            in_specs=[pl.BlockSpec(memory_space=pltpu.VMEM)] * ys + [anywhere],
-            out_specs=anywhere,
-            scratch_shapes=[pltpu.SemaphoreType.DMA((ys,))],
-        ),
-        input_output_aliases={ys + 1: 0},
-    )(light_counts, *passed, light_out.reshape(zs, ys, BLOCK, D))
+    light_out = local_call(
+        hand_on_kernel, [light_counts], [*passed, light_out.reshape(zs, ys, BLOCK, D)], [(zs, ys, BLOCK, D)],
+        [pltpu.SemaphoreType.DMA((ys,))], hbm=ys,
+    )[0]
     light_out = spread(light_out.reshape(zs * ys, BLOCK, D))
     return local_call(functools.partial(post_kernel, zs), [table], [light_out], [queries.shape])[0]
 

time: 182 us -> 178 us (0.978)
  waiting for transfers between devices: 57.1 us -> 53.5 us
  local copies, waits for them, and re-layouts: 8.81 us -> 12 us
  blocking collectives: 42.7 us -> 39.9 us
    ppermute x3 -> x4, waiting for transfers between devices: 44.7 us -> 33.3 us  [over_y(): return lax.ppermute(x, 'split', [(i, (i + dy) % ys) for i in range(ys)])]
    all_to_all x1, waiting for transfers between devices: 1.95 us -> 10.8 us  [spread(): lax.all_to_all(x, ('z', 'split'), split_axis=0, concat_axis=0, tiled=True)]
    all_to_all x1, blocking collectives: 42.7 us -> 39.9 us  [spread(): lax.all_to_all(x, ('z', 'split'), split_axis=0, concat_axis=0, tiled=True)]
    pallas_call x1 -> x0, Pallas kernels: 1.88 us -> none  [body(): pl.pallas_call(hand_on_kernel, out_shape=jax.ShapeDtypeStruct((zs, ys, BL...]
    pallas_call x5 -> x6, Pallas kernels: 37.5 us -> 38.9 us  [local_call(): pl.pallas_call(kernel, out_shape=[jax.ShapeDtypeStruct(x, jnp.bfloat16) f...]
    ppermute x3 -> x4, starting transfers between devices: 4.78 us -> 4.75 us  [over_y(): return lax.ppermute(x, 'split', [(i, (i + dy) % ys) for i in range(ys)])]
  transfers between devices with their start and end apart: 13 -> 15, of which waited for: 5 -> 7; matrix products, arithmetic and copies ran while one was open for 4% -> 6% of each run, Pallas kernels for 17% -> 17%
where the time goes in v3:
time: 178 us; the launch traced here: 177 us
  waiting for transfers between devices  53.5 us (30%)
  blocking collectives  39.9 us (22%)
  Pallas kernels  38.9 us (22%)
  starting transfers between devices  26.1 us (15%)
  local copies, waits for them, and re-layouts  12 us (7%)
  between operations  4.31 us (2%)
  other arithmetic  2.47 us (1%)
    all_to_all x1, blocking collectives, spread(): lax.all_to_all(x, ('z', 'split'), split_axis=0, concat_axis=0, tiled=True)  39.9 us
    pallas_call x6, Pallas kernels, local_call(): pl.pallas_call(kernel, out_shape=[jax.ShapeDtypeStruct(x, jnp.bfloat16) f...  38.9 us
    ppermute x4, waiting for transfers between devices, over_y(): return lax.ppermute(x, 'split', [(i, (i + dy) % ys) for i in range(ys)])  33.3 us
    all_to_all x1, waiting for transfers between devices, spread(): lax.all_to_all(x, ('z', 'split'), split_axis=0, concat_axis=0, tiled=True)  10.8 us
    all_to_all x1, starting transfers between devices, body(): wide = lax.all_to_all(wide, 'z', split_axis=0, concat_axis=0, tiled=True)  8.48 us
    all_to_all x1, waiting for transfers between devices, body(): wide = lax.all_to_all(wide, 'z', split_axis=0, concat_axis=0, tiled=True)  8.22 us
    ppermute x3, starting transfers between devices, body(): lax.ppermute(wide_out, 'split', [(i, used)])  7.23 us
    all_to_all x1, starting transfers between devices, spread(): lax.all_to_all(x, ('z', 'split'), split_axis=0, concat_axis=0, tiled=True)  5.08 us
  transfers between devices with their start and end apart: 15, of which 7 were waited for; matrix products, arithmetic and copies ran while one was open for 6% of the time, Pallas kernels for 17%

profile of v3, /device:TPU:12, one launch (start us, length us, event | category | flops | bytes accessed | tf_op | source)
XLA Modules:
  0.0 177.2 jit_solution(14379939183518526804)
XLA Ops:
  0.0 0.8 reduce_sum.27
  1.2 0.7 select_reduce_fusion.tab
  1.9 3.0 %shard_map.55 = bf16[8,3,128,128]{3,2,1,0:T(8,128)(2,1)} custom-call(s32[32]{0:T(128)} %select_reduce_fusion.tab, bf16[128,4096]{1,0:T(8,128)(2,1)} %q_ref.3, bf16[128,4096]{1,0:T(8,128)(2,1)} %k_ref.3, bf16[128,4096]{1,0:T(8,128)(2,1)} %v_ref.3), custom_call_target="tpu_custom_call" | custom-call | tf_op jit(solution)/shard_map/pallas_call | solution.py:218
  4.9 8.5 %all-to-all-start = ((bf16[8,3,128,128]{3,2,1,0:T(8,128)(2,1)}), bf16[8,3,128,128]{3,2,1,0:T(8,128)(2,1)S(1)}, u32[]{:S(2)}, u32[]{:S(2)}) async-start(bf16[8,3,128,128]{3,2,1,0:T(8,128)(2,1)} %shard_map.55), calls=%async_computation | async-start | bytes 1572864 | tf_op jit(solution)/shard_map/all_to_all | solution.py:282
  13.3 0.7 fusion.33
  16.8 4.8 %shard_map.56 = bf16[32,3,128,128]{3,2,1,0:T(8,128)(2,1)} custom-call(s32[32]{0:T(128)} %select_reduce_fusion.tab, bf16[128,4096]{1,0:T(8,128)(2,1)} %q_ref.3, bf16[128,4096]{1,0:T(8,128)(2,1)} %k_ref.3, bf16[128,4096]{1,0:T(8,128)(2,1)} %v_ref.3), custom_call_target="tpu_custom_call" | custom-call | tf_op jit(solution)/shard_map/pallas_call | solution.py:218
  23.0 0.7 fusion.28
  23.7 0.7 gather_fusion.3
  24.4 0.8 dynamic-slice_bitcast_fusion
  25.8 1.2 gather_fusion.1
  28.2 8.2 %all-to-all-done.q_hbm = bf16[8,3,128,128]{3,2,1,0:T(8,128)(2,1)S(1)} async-done(((bf16[8,3,128,128]{3,2,1,0:T(8,128)(2,1)}), bf16[8,3,128,128]{3,2,1,0:T(8,128)(2,1)S(1)}, u32[]{:S(2)}, u32[]{:S(2)}) %all-to-all-start) | async-done | bytes 786464 | tf_op jit(solution)/shard_map/all_to_all | solution.py:282
  36.5 0.9 copy-done.1
  37.3 5.1 %all-to-all-start.1 = ((bf16[32,3,128,128]{3,2,1,0:T(8,128)(2,1)}), bf16[32,3,128,128]{3,2,1,0:T(8,128)(2,1)S(1)}, u32[]{:S(2)}, u32[]{:S(2)}) async-start(bf16[32,3,128,128]{3,2,1,0:T(8,128)(2,1)} %shard_map.56), calls=%async_computation.1 | async-start | bytes 6291456 | tf_op jit(solution)/shard_map/all_to_all | solution.py:277
  42.4 1.9 %slice_bitcast_fusion.refs_0_ = bf16[2,8,128,128]{3,2,1,0:T(8,128)(2,1)} fusion(bf16[8,3,128,128]{3,2,1,0:T(8,128)(2,1)} %copy-done.1), kind=kLoop, calls=%fused_computation.4 | loop fusion | bytes 1048576 | tf_op jit(solution)/shard_map/transpose | solution.py:286
  44.6 1.8 %collective-permute-start = (bf16[2,8,128,128]{3,2,1,0:T(8,128)(2,1)}, bf16[2,8,128,128]{3,2,1,0:T(8,128)(2,1)}, u32[]{:S(2)}, u32[]{:S(2)}) collective-permute-start(bf16[2,8,128,128]{3,2,1,0:T(8,128)(2,1)} %slice_bitcast_fusion.refs_0_), channel_id=1, source_target_pairs={{0,1},{1,2},{2,3},{3,0},{4,5},{5,6},{6,7},{7,4},{8,9},{9,10},{10,1... | collective-permute-start | bytes 1572872 | tf_op jit(solution)/shard_map/ppermute | solution.py:289
  46.3 26.2 %collective-permute-done.1.refs_2_ = bf16[2,8,128,128]{3,2,1,0:T(8,128)(2,1)} collective-permute-done((bf16[2,8,128,128]{3,2,1,0:T(8,128)(2,1)}, bf16[2,8,128,128]{3,2,1,0:T(8,128)(2,1)}, u32[]{:S(2)}, u32[]{:S(2)}) %collective-permute-start.1) | collective-permute-done | bytes 524320 | tf_op jit(solution)/shard_map/ppermute | solution.py:289
  72.5 1.0 slice_bitcast_fusion.1
  73.5 2.5 %collective-permute-start.3 = (bf16[8,128,128]{2,1,0:T(8,128)(2,1)S(1)}, bf16[8,128,128]{2,1,0:T(8,128)(2,1)S(1)}, u32[]{:S(2)}, u32[]{:S(2)}) collective-permute-start(bf16[8,128,128]{2,1,0:T(8,128)(2,1)S(1)} %slice_bitcast_fusion.1), channel_id=1, source_target_pairs={{0,3},{1,0},{2,1},{3,2},{4,7},{5,4},{6,5},{7,6},{8,11},{9,8},{10,9... | collective-permute-start | bytes 786440 | tf_op jit(solution)/shard_map/ppermute | solution.py:289
  76.0 1.0 slice_bitcast_fusion.2
  77.7 6.4 %collective-permute-done.3.refs_4_ = bf16[8,128,128]{2,1,0:T(8,128)(2,1)S(1)} collective-permute-done((bf16[8,128,128]{2,1,0:T(8,128)(2,1)S(1)}, bf16[8,128,128]{2,1,0:T(8,128)(2,1)S(1)}, u32[]{:S(2)}, u32[]{:S(2)}) %collective-permute-start.3) | collective-permute-done | bytes 262176 | tf_op jit(solution)/shard_map/ppermute | solution.py:289
  85.8 0.9 collective-permute-done.7.refs_8_
  86.7 16.4 %shard_map.57.refs_3_ = bf16[8,128,128]{2,1,0:T(8,128)(2,1)} custom-call(s32[512]{0:T(512)} %reshape.115.lists, s32[8]{0:T(128)} %gather_fusion.1, bf16[8,3,128,128]{3,2,1,0:T(8,128)(2,1)} %copy-done.1, bf16[2,8,128,128]{3,2,1,0:T(8,128)(2,1)} %slice_bitcast_fusion.refs_0_, bf16[2,8,128,128]{3,2,1,0:T(8,128)(2,1)} %collective-permute-done.refs_1_, ...), custom_call_target="tpu_custom_call" | custom-call | tf_op jit(solution)/shard_map/pallas_call | solution.py:218
  103.1 10.8 %all-to-all-done.1.own = bf16[32,3,128,128]{3,2,1,0:T(8,128)(2,1)S(1)} async-done(((bf16[32,3,128,128]{3,2,1,0:T(8,128)(2,1)}), bf16[32,3,128,128]{3,2,1,0:T(8,128)(2,1)S(1)}, u32[]{:S(2)}, u32[]{:S(2)}) %all-to-all-start.1) | async-done | bytes 3145760 | tf_op jit(solution)/shard_map/all_to_all | solution.py:277
  113.9 0.7 collective-permute-start.11
  114.6 5.2 %collective-permute-start.10 = (bf16[8,128,128]{2,1,0:T(8,128)(2,1)}, bf16[8,128,128]{2,1,0:T(8,128)(2,1)}, u32[]{:S(2)}, u32[]{:S(2)}) collective-permute-start(bf16[8,128,128]{2,1,0:T(8,128)(2,1)} %shard_map.57.refs_3_), channel_id=1, source_target_pairs={{1,3},{5,7},{9,11},{13,15},{17,19},{21,23},{25,27},{29,31},{33,35}... | collective-permute-start | bytes 786440 | tf_op jit(solution)/shard_map/ppermute | solution.py:315
  119.8 1.4 collective-permute-start.9
  121.1 0.7 reshape.116.lists
  121.8 8.6 %shard_map.58 = bf16[32,128,128]{2,1,0:T(8,128)(2,1)} custom-call(s32[2048]{0:T(1024)} %reshape.116.lists, s32[32]{0:T(128)} %broadcast_select_fusion.counts, bf16[32,3,128,128]{3,2,1,0:T(8,128)(2,1)} %copy-done, bf16[32,3,128,128]{3,2,1,0:T(8,128)(2,1)} %collective-permute-done.12.other), custom_call_target="tpu_custom_call" | custom-call | tf_op jit(solution)/shard_map/pallas_call | solution.py:218
  130.5 0.7 copy-done.3
  131.2 3.0 %shard_map.59 = bf16[8,4,128,128]{3,2,1,0:T(8,128)(2,1)} custom-call(s32[32]{0:T(128)} %broadcast_select_fusion.counts, bf16[8,128,128]{2,1,0:T(8,128)(2,1)} %collective-permute-done.9.refs_0_, bf16[8,128,128]{2,1,0:T(8,128)(2,1)} %collective-permute-done.10.refs_1_, bf16[8,128,128]{2,1,0:T(8,128)(2,1)} %copy-done.3, ...), custom_call_target="tpu_custom_call" | custom-call | tf_op jit(solution)/shard_map/pallas_call | solution.py:218
  134.2 39.9 %all_to_all.15.light = bf16[32,128,128]{2,1,0:T(8,128)(2,1)} all-to-all(bf16[32,128,128]{2,1,0:T(8,128)(2,1)} %bitcast.22), channel_id=1, replica_groups=mesh['clip'=4,'z'=8,'core'=2,'split'=4] {'z','split'}, dimensions={0} | all-to-all | bytes 2097152 | tf_op jit(solution)/shard_map/all_to_all | solution.py:277
  174.0 3.1 %shard_map.60 = bf16[128,4096]{1,0:T(8,128)(2,1)} custom-call(s32[32]{0:T(128)} %select_reduce_fusion.tab, bf16[32,128,128]{2,1,0:T(8,128)(2,1)} %all_to_all.15.light), custom_call_target="tpu_custom_call" | custom-call | tf_op jit(solution)/shard_map/pallas_call | solution.py:218
  (42 shorter events, 4.8 us)
Async XLA Ops:
  1.9 11.5 %copy-start.4 = (s32[32]{0:T(128)S(1)}, s32[32]{0:T(128)}, u32[]{:S(2)}) copy-start(s32[32]{0:T(128)} %select_reduce_fusion.tab) | copy-start | bytes 388
  4.9 31.6 %all-to-all-start = ((bf16[8,3,128,128]{3,2,1,0:T(8,128)(2,1)}), bf16[8,3,128,128]{3,2,1,0:T(8,128)(2,1)S(1)}, u32[]{:S(2)}, u32[]{:S(2)}) async-start(bf16[8,3,128,128]{3,2,1,0:T(8,128)(2,1)} %shard_map.55), calls=%async_computation | async-start | bytes 1572864 | tf_op jit(solution)/shard_map/all_to_all | solution.py:282
  36.5 0.9 copy-start.1
  37.3 76.6 %all-to-all-start.1 = ((bf16[32,3,128,128]{3,2,1,0:T(8,128)(2,1)}), bf16[32,3,128,128]{3,2,1,0:T(8,128)(2,1)S(1)}, u32[]{:S(2)}, u32[]{:S(2)}) async-start(bf16[32,3,128,128]{3,2,1,0:T(8,128)(2,1)} %shard_map.56), calls=%async_computation.1 | async-start | bytes 6291456 | tf_op jit(solution)/shard_map/all_to_all | solution.py:277
  44.3 28.2 %collective-permute-start.1 = (bf16[2,8,128,128]{3,2,1,0:T(8,128)(2,1)}, bf16[2,8,128,128]{3,2,1,0:T(8,128)(2,1)}, u32[]{:S(2)}, u32[]{:S(2)}) collective-permute-start(bf16[2,8,128,128]{3,2,1,0:T(8,128)(2,1)} %slice_bitcast_fusion.refs_0_), channel_id=1, source_target_pairs={{0,3},{1,0},{2,1},{3,2},{4,7},{5,4},{6,5},{7,6},{8,11},{9,8},{10,9... | collective-permute-start | bytes 1572872 | tf_op jit(solution)/shard_map/ppermute | solution.py:289
  44.6 31.5 %collective-permute-start = (bf16[2,8,128,128]{3,2,1,0:T(8,128)(2,1)}, bf16[2,8,128,128]{3,2,1,0:T(8,128)(2,1)}, u32[]{:S(2)}, u32[]{:S(2)}) collective-permute-start(bf16[2,8,128,128]{3,2,1,0:T(8,128)(2,1)} %slice_bitcast_fusion.refs_0_), channel_id=1, source_target_pairs={{0,1},{1,2},{2,3},{3,0},{4,5},{5,6},{6,7},{7,4},{8,9},{9,10},{10,1... | collective-permute-start | bytes 1572872 | tf_op jit(solution)/shard_map/ppermute | solution.py:289
  46.3 39.1 %collective-permute-start.4 = (bf16[2,8,128,128]{3,2,1,0:T(8,128)(2,1)}, bf16[2,8,128,128]{3,2,1,0:T(8,128)(2,1)}, u32[]{:S(2)}, u32[]{:S(2)}) collective-permute-start(bf16[2,8,128,128]{3,2,1,0:T(8,128)(2,1)} %slice_bitcast_fusion.refs_0_), channel_id=1, source_target_pairs={{0,4},{4,0},{1,5},{5,1},{2,6},{6,2},{3,7},{7,3},{8,12},{12,8},{9,1... | collective-permute-start | bytes 1572872 | tf_op jit(solution)/shard_map/ppermute | solution.py:280
  73.5 10.6 %collective-permute-start.3 = (bf16[8,128,128]{2,1,0:T(8,128)(2,1)S(1)}, bf16[8,128,128]{2,1,0:T(8,128)(2,1)S(1)}, u32[]{:S(2)}, u32[]{:S(2)}) collective-permute-start(bf16[8,128,128]{2,1,0:T(8,128)(2,1)S(1)} %slice_bitcast_fusion.1), channel_id=1, source_target_pairs={{0,3},{1,0},{2,1},{3,2},{4,7},{5,4},{6,5},{7,6},{8,11},{9,8},{10,9... | collective-permute-start | bytes 786440 | tf_op jit(solution)/shard_map/ppermute | solution.py:289
  77.0 7.8 %collective-permute-start.2 = (bf16[8,128,128]{2,1,0:T(8,128)(2,1)S(1)}, bf16[8,128,128]{2,1,0:T(8,128)(2,1)}, u32[]{:S(2)}, u32[]{:S(2)}) collective-permute-start(bf16[8,128,128]{2,1,0:T(8,128)(2,1)S(1)} %slice_bitcast_fusion.2), channel_id=1, source_target_pairs={{0,1},{1,2},{2,3},{3,0},{4,5},{5,6},{6,7},{7,4},{8,9},{9,10},{10,1... | collective-permute-start | bytes 786440 | tf_op jit(solution)/shard_map/ppermute | solution.py:289
  77.2 9.5 %collective-permute-start.6 = (bf16[2,8,128,128]{3,2,1,0:T(8,128)(2,1)}, bf16[2,8,128,128]{3,2,1,0:T(8,128)(2,1)}, u32[]{:S(2)}, u32[]{:S(2)}) collective-permute-start(bf16[2,8,128,128]{3,2,1,0:T(8,128)(2,1)} %collective-permute-done.1.refs_2_), channel_id=1, source_target_pairs={{0,4},{4,0},{1,5},{5,1},{2,6},{6,2},{3,7},{7,3},{8,12},{12,8},{9,1... | collective-permute-start | bytes 1572872 | tf_op jit(solution)/shard_map/ppermute | solution.py:280
  77.2 9.5 %collective-permute-start.5 = (bf16[2,8,128,128]{3,2,1,0:T(8,128)(2,1)}, bf16[2,8,128,128]{3,2,1,0:T(8,128)(2,1)}, u32[]{:S(2)}, u32[]{:S(2)}) collective-permute-start(bf16[2,8,128,128]{3,2,1,0:T(8,128)(2,1)} %collective-permute-done.refs_1_), channel_id=1, source_target_pairs={{0,4},{4,0},{1,5},{5,1},{2,6},{6,2},{3,7},{7,3},{8,12},{12,8},{9,1... | collective-permute-start | bytes 1572872 | tf_op jit(solution)/shard_map/ppermute | solution.py:280
  84.2 2.5 %copy-start.2 = (bf16[8,128,128]{2,1,0:T(8,128)(2,1)}, bf16[8,128,128]{2,1,0:T(8,128)(2,1)S(1)}, u32[]{:S(2)}) copy-start(bf16[8,128,128]{2,1,0:T(8,128)(2,1)S(1)} %collective-permute-done.3.refs_4_) | copy-start | bytes 786436
  84.2 1.7 collective-permute-start.8
  84.8 1.9 %collective-permute-start.7 = (bf16[8,128,128]{2,1,0:T(8,128)(2,1)}, bf16[8,128,128]{2,1,0:T(8,128)(2,1)}, u32[]{:S(2)}, u32[]{:S(2)}) collective-permute-start(bf16[8,128,128]{2,1,0:T(8,128)(2,1)} %collective-permute-done.2.refs_3_), channel_id=1, source_target_pairs={{0,4},{4,0},{1,5},{5,1},{2,6},{6,2},{3,7},{7,3},{8,12},{12,8},{9,1... | collective-permute-start | bytes 786440 | tf_op jit(solution)/shard_map/ppermute | solution.py:280
  113.9 7.9 %copy-start = (bf16[32,3,128,128]{3,2,1,0:T(8,128)(2,1)}, bf16[32,3,128,128]{3,2,1,0:T(8,128)(2,1)S(1)}, u32[]{:S(2)}) copy-start(bf16[32,3,128,128]{3,2,1,0:T(8,128)(2,1)S(1)} %all-to-all-done.1.own) | copy-start | bytes 9437188
  113.9 7.9 %collective-permute-start.12 = (bf16[32,3,128,128]{3,2,1,0:T(8,128)(2,1)S(1)}, bf16[32,3,128,128]{3,2,1,0:T(8,128)(2,1)}, u32[]{:S(2)}, u32[]{:S(2)}) collective-permute-start(bf16[32,3,128,128]{3,2,1,0:T(8,128)(2,1)S(1)} %all-to-all-done.1.own), channel_id=1, source_target_pairs={{0,4},{4,0},{1,5},{5,1},{2,6},{6,2},{3,7},{7,3},{8,12},{12,8},{9,1... | collective-permute-start | bytes 9437192 | tf_op jit(solution)/shard_map/ppermute | solution.py:280
  113.9 16.5 %collective-permute-start.11 = (bf16[8,128,128]{2,1,0:T(8,128)(2,1)}, bf16[8,128,128]{2,1,0:T(8,128)(2,1)S(1)}, u32[]{:S(2)}, u32[]{:S(2)}) collective-permute-start(bf16[8,128,128]{2,1,0:T(8,128)(2,1)} %shard_map.57.refs_3_), channel_id=1, source_target_pairs={{2,3},{6,7},{10,11},{14,15},{18,19},{22,23},{26,27},{30,31},{34,35... | collective-permute-start | bytes 786440 | tf_op jit(solution)/shard_map/ppermute | solution.py:315
  114.6 15.9 %collective-permute-start.10 = (bf16[8,128,128]{2,1,0:T(8,128)(2,1)}, bf16[8,128,128]{2,1,0:T(8,128)(2,1)}, u32[]{:S(2)}, u32[]{:S(2)}) collective-permute-start(bf16[8,128,128]{2,1,0:T(8,128)(2,1)} %shard_map.57.refs_3_), channel_id=1, source_target_pairs={{1,3},{5,7},{9,11},{13,15},{17,19},{21,23},{25,27},{29,31},{33,35}... | collective-permute-start | bytes 786440 | tf_op jit(solution)/shard_map/ppermute | solution.py:315
  119.8 10.7 %collective-permute-start.9 = (bf16[8,128,128]{2,1,0:T(8,128)(2,1)}, bf16[8,128,128]{2,1,0:T(8,128)(2,1)}, u32[]{:S(2)}, u32[]{:S(2)}) collective-permute-start(bf16[8,128,128]{2,1,0:T(8,128)(2,1)} %shard_map.57.refs_3_), channel_id=1, source_target_pairs={{0,3},{4,7},{8,11},{12,15},{16,19},{20,23},{24,27},{28,31},{32,35}... | collective-permute-start | bytes 786440 | tf_op jit(solution)/shard_map/ppermute | solution.py:315
  130.5 0.7 copy-start.3

commit v4 on v3

--- a/solution.py
+++ b/solution.py
@@ -40,11 +40,11 @@
                 light[r * columns + y, i] = col(ref, head)
 
 
-def post_kernel(rows, tab, light, out):
+def post_kernel(rows, tab, wide, light, out):
     columns = light.shape[0] // rows
     used = tab.shape[0] // rows - 1
     for r in range(rows):
-        out[:, pl.ds(pl.multiple_of(tab[r] * D, D), D)] = light[r * columns + used]
+        out[:, pl.ds(pl.multiple_of(tab[r] * D, D), D)] = wide[r]
         for y in range(used):
             at = pl.ds(pl.multiple_of(tab[rows + r * used + y] * D, D), D)
             out[:, at] = light[r * columns + y]
@@ -164,22 +164,6 @@
         o_ref[r] = x
 
     attend_head(lists, counts, 0, lambda r: q_ref[r], kv, put)
-
-
-def hand_on_kernel(counts, *refs):
-    passed, (light, out, sems) = refs[:-3], refs[-3:]
-
-    @pl.when(counts[0] == 0)
-    def place():
-        copies = [pltpu.make_async_copy(ref, out.at[:, y], sems.at[y]) for y, ref in enumerate(passed)]
-        for copy in copies:
-            copy.start()
-        for copy in copies:
-            copy.wait()
-
-    @pl.when(counts[0] > 0)
-    def keep():
-        out[...] = light[...]
 
 
 def light_kernel(total, lists, counts, own, other, o_ref, q_ref, kv, sems):
@@ -312,13 +296,10 @@
         ],
         hbm=2,
     )[0]
-    passed = [lax.ppermute(wide_out, "split", [(i, used)]) for i in range(used)] + [wide_out]
-    light_out = local_call(
-        hand_on_kernel, [light_counts], [*passed, light_out.reshape(zs, ys, BLOCK, D)], [(zs, ys, BLOCK, D)],
-        [pltpu.SemaphoreType.DMA((ys,))], hbm=ys,
-    )[0]
-    light_out = spread(light_out.reshape(zs * ys, BLOCK, D))
-    return local_call(functools.partial(post_kernel, zs), [table], [light_out], [queries.shape])[0]
+    wide_out = lax.all_to_all(wide_out, "z", split_axis=0, concat_axis=0, tiled=True)
+    return local_call(
+        functools.partial(post_kernel, zs), [table], [wide_out, spread(light_out)], [queries.shape]
+    )[0]
 
 
 def solution(mesh):

time: 178 us -> 170 us (0.955)
  blocking collectives: 39.9 us -> 35.4 us
  waiting for transfers between devices: 53.5 us -> 57.3 us
  starting transfers between devices: 26.1 us -> 22.9 us
  Pallas kernels: 38.9 us -> 36 us
    ppermute x3 -> x0, starting transfers between devices: 7.23 us -> none  [body(): lax.ppermute(wide_out, 'split', [(i, used)])]
    all_to_all x1, blocking collectives: 39.9 us -> 35.4 us  [spread(): lax.all_to_all(x, ('z', 'split'), split_axis=0, concat_axis=0, tiled=True)]
    all_to_all x0 -> x1, starting transfers between devices: none -> 4.03 us  [body(): lax.all_to_all(wide_out, 'z', split_axis=0, concat_axis=0, tiled=True)]
    pallas_call x6 -> x5, Pallas kernels: 38.9 us -> 36 us  [local_call(): pl.pallas_call(kernel, out_shape=[jax.ShapeDtypeStruct(x, jnp.bfloat16) f...]
    all_to_all x0 -> x1, waiting for transfers between devices: none -> 2.13 us  [body(): lax.all_to_all(wide_out, 'z', split_axis=0, concat_axis=0, tiled=True)]
  transfers between devices with their start and end apart: 15 -> 13, of which waited for: 7 -> 9; matrix products, arithmetic and copies ran while one was open for 6% -> 6% of each run, Pallas kernels for 17% -> 18%
where the time goes in v4:
time: 170 us; the launch traced here: 169 us
  waiting for transfers between devices  57.3 us (34%)
  Pallas kernels  36 us (21%)
  blocking collectives  35.4 us (21%)
  starting transfers between devices  22.9 us (13%)
  local copies, waits for them, and re-layouts  11.3 us (7%)
  between operations  3.86 us (2%)
  other arithmetic  2.42 us (1%)
    pallas_call x5, Pallas kernels, local_call(): pl.pallas_call(kernel, out_shape=[jax.ShapeDtypeStruct(x, jnp.bfloat16) f...  36 us
    all_to_all x1, blocking collectives, spread(): lax.all_to_all(x, ('z', 'split'), split_axis=0, concat_axis=0, tiled=True)  35.4 us
    ppermute x4, waiting for transfers between devices, over_y(): return lax.ppermute(x, 'split', [(i, (i + dy) % ys) for i in range(ys)])  33.3 us
    all_to_all x1, waiting for transfers between devices, spread(): lax.all_to_all(x, ('z', 'split'), split_axis=0, concat_axis=0, tiled=True)  10.8 us
    all_to_all x1, waiting for transfers between devices, body(): wide = lax.all_to_all(wide, 'z', split_axis=0, concat_axis=0, tiled=True)  8.73 us
    all_to_all x1, starting transfers between devices, body(): wide = lax.all_to_all(wide, 'z', split_axis=0, concat_axis=0, tiled=True)  8.48 us
    all_to_all x1, starting transfers between devices, spread(): lax.all_to_all(x, ('z', 'split'), split_axis=0, concat_axis=0, tiled=True)  5.08 us
    ppermute x4, starting transfers between devices, over_y(): return lax.ppermute(x, 'split', [(i, (i + dy) % ys) for i in range(ys)])  4.75 us
  transfers between devices with their start and end apart: 13, of which 9 were waited for; matrix products, arithmetic and copies ran while one was open for 6% of the time, Pallas kernels for 18%

profile of v4, /device:TPU:12, one launch (start us, length us, event | category | flops | bytes accessed | tf_op | source)
XLA Modules:
  0.0 169.1 jit_solution(8592013930251279270)
XLA Ops:
  0.0 0.8 reduce_sum.27
  1.2 0.7 select_reduce_fusion.tab
  1.9 3.0 %shard_map.55 = bf16[8,3,128,128]{3,2,1,0:T(8,128)(2,1)} custom-call(s32[32]{0:T(128)} %select_reduce_fusion.tab, bf16[128,4096]{1,0:T(8,128)(2,1)} %q_ref.3, bf16[128,4096]{1,0:T(8,128)(2,1)} %k_ref.3, bf16[128,4096]{1,0:T(8,128)(2,1)} %v_ref.3), custom_call_target="tpu_custom_call" | custom-call | tf_op jit(solution)/shard_map/pallas_call | solution.py:202
  4.9 8.5 %all-to-all-start = ((bf16[8,3,128,128]{3,2,1,0:T(8,128)(2,1)}), bf16[8,3,128,128]{3,2,1,0:T(8,128)(2,1)S(1)}, u32[]{:S(2)}, u32[]{:S(2)}) async-start(bf16[8,3,128,128]{3,2,1,0:T(8,128)(2,1)} %shard_map.55), calls=%async_computation | async-start | bytes 1572864 | tf_op jit(solution)/shard_map/all_to_all | solution.py:266
  13.4 0.7 fusion.33
  16.6 4.8 %shard_map.56 = bf16[32,3,128,128]{3,2,1,0:T(8,128)(2,1)} custom-call(s32[32]{0:T(128)} %select_reduce_fusion.tab, bf16[128,4096]{1,0:T(8,128)(2,1)} %q_ref.3, bf16[128,4096]{1,0:T(8,128)(2,1)} %k_ref.3, bf16[128,4096]{1,0:T(8,128)(2,1)} %v_ref.3), custom_call_target="tpu_custom_call" | custom-call | tf_op jit(solution)/shard_map/pallas_call | solution.py:202
  22.6 0.7 fusion.28
  23.3 0.7 gather_fusion.3
  24.0 0.8 dynamic-slice_bitcast_fusion
  25.4 1.2 gather_fusion.1
  27.8 8.7 %all-to-all-done.q_hbm = bf16[8,3,128,128]{3,2,1,0:T(8,128)(2,1)S(1)} async-done(((bf16[8,3,128,128]{3,2,1,0:T(8,128)(2,1)}), bf16[8,3,128,128]{3,2,1,0:T(8,128)(2,1)S(1)}, u32[]{:S(2)}, u32[]{:S(2)}) %all-to-all-start) | async-done | bytes 786464 | tf_op jit(solution)/shard_map/all_to_all | solution.py:266
  36.5 0.9 copy-done.1
  37.4 5.1 %all-to-all-start.1 = ((bf16[32,3,128,128]{3,2,1,0:T(8,128)(2,1)}), bf16[32,3,128,128]{3,2,1,0:T(8,128)(2,1)S(1)}, u32[]{:S(2)}, u32[]{:S(2)}) async-start(bf16[32,3,128,128]{3,2,1,0:T(8,128)(2,1)} %shard_map.56), calls=%async_computation.1 | async-start | bytes 6291456 | tf_op jit(solution)/shard_map/all_to_all | solution.py:261
  42.5 1.9 %slice_bitcast_fusion.refs_0_ = bf16[2,8,128,128]{3,2,1,0:T(8,128)(2,1)} fusion(bf16[8,3,128,128]{3,2,1,0:T(8,128)(2,1)} %copy-done.1), kind=kLoop, calls=%fused_computation.4 | loop fusion | bytes 1048576 | tf_op jit(solution)/shard_map/transpose | solution.py:270
  44.6 1.8 %collective-permute-start = (bf16[2,8,128,128]{3,2,1,0:T(8,128)(2,1)}, bf16[2,8,128,128]{3,2,1,0:T(8,128)(2,1)}, u32[]{:S(2)}, u32[]{:S(2)}) collective-permute-start(bf16[2,8,128,128]{3,2,1,0:T(8,128)(2,1)} %slice_bitcast_fusion.refs_0_), channel_id=1, source_target_pairs={{0,1},{1,2},{2,3},{3,0},{4,5},{5,6},{6,7},{7,4},{8,9},{9,10},{10,1... | collective-permute-start | bytes 1572872 | tf_op jit(solution)/shard_map/ppermute | solution.py:273
  46.4 26.2 %collective-permute-done.1.refs_2_ = bf16[2,8,128,128]{3,2,1,0:T(8,128)(2,1)} collective-permute-done((bf16[2,8,128,128]{3,2,1,0:T(8,128)(2,1)}, bf16[2,8,128,128]{3,2,1,0:T(8,128)(2,1)}, u32[]{:S(2)}, u32[]{:S(2)}) %collective-permute-start.1) | collective-permute-done | bytes 524320 | tf_op jit(solution)/shard_map/ppermute | solution.py:273
  72.6 1.0 slice_bitcast_fusion.1
  73.6 2.5 %collective-permute-start.3 = (bf16[8,128,128]{2,1,0:T(8,128)(2,1)S(1)}, bf16[8,128,128]{2,1,0:T(8,128)(2,1)S(1)}, u32[]{:S(2)}, u32[]{:S(2)}) collective-permute-start(bf16[8,128,128]{2,1,0:T(8,128)(2,1)S(1)} %slice_bitcast_fusion.1), channel_id=1, source_target_pairs={{0,3},{1,0},{2,1},{3,2},{4,7},{5,4},{6,5},{7,6},{8,11},{9,8},{10,9... | collective-permute-start | bytes 786440 | tf_op jit(solution)/shard_map/ppermute | solution.py:273
  76.1 1.0 slice_bitcast_fusion.2
  77.8 6.4 %collective-permute-done.3.refs_4_ = bf16[8,128,128]{2,1,0:T(8,128)(2,1)S(1)} collective-permute-done((bf16[8,128,128]{2,1,0:T(8,128)(2,1)S(1)}, bf16[8,128,128]{2,1,0:T(8,128)(2,1)S(1)}, u32[]{:S(2)}, u32[]{:S(2)}) %collective-permute-start.3) | collective-permute-done | bytes 262176 | tf_op jit(solution)/shard_map/ppermute | solution.py:273
  84.2 0.6 collective-permute-done.2.refs_3_
  84.9 0.7 reshape.109.lists
  85.9 0.9 collective-permute-done.7.refs_8_
  86.7 16.4 %shard_map.57 = bf16[8,128,128]{2,1,0:T(8,128)(2,1)} custom-call(s32[512]{0:T(512)} %reshape.109.lists, s32[8]{0:T(128)} %gather_fusion.1, bf16[8,3,128,128]{3,2,1,0:T(8,128)(2,1)} %copy-done.1, bf16[2,8,128,128]{3,2,1,0:T(8,128)(2,1)} %slice_bitcast_fusion.refs_0_, bf16[2,8,128,128]{3,2,1,0:T(8,128)(2,1)} %collective-permute-done.refs_1_, ...), custom_call_target="tpu_custom_call" | custom-call | tf_op jit(solution)/shard_map/pallas_call | solution.py:202
  103.1 10.8 %all-to-all-done.1.own = bf16[32,3,128,128]{3,2,1,0:T(8,128)(2,1)S(1)} async-done(((bf16[32,3,128,128]{3,2,1,0:T(8,128)(2,1)}), bf16[32,3,128,128]{3,2,1,0:T(8,128)(2,1)S(1)}, u32[]{:S(2)}, u32[]{:S(2)}) %all-to-all-start.1) | async-done | bytes 3145760 | tf_op jit(solution)/shard_map/all_to_all | solution.py:261
  114.0 4.0 %all-to-all-start.2 = ((bf16[8,128,128]{2,1,0:T(8,128)(2,1)}), bf16[8,128,128]{2,1,0:T(8,128)(2,1)S(1)}, u32[]{:S(2)}, u32[]{:S(2)}) async-start(bf16[8,128,128]{2,1,0:T(8,128)(2,1)} %shard_map.57), calls=%async_computation.2 | async-start | bytes 524288 | tf_op jit(solution)/shard_map/all_to_all | solution.py:299
  118.0 0.7 reshape.110.lists
  118.6 1.1 collective-permute-done.9.other
  119.7 8.6 %shard_map.58 = bf16[32,128,128]{2,1,0:T(8,128)(2,1)} custom-call(s32[2048]{0:T(1024)} %reshape.110.lists, s32[32]{0:T(128)} %broadcast_select_fusion.counts, bf16[32,3,128,128]{3,2,1,0:T(8,128)(2,1)} %copy-done, bf16[32,3,128,128]{3,2,1,0:T(8,128)(2,1)} %collective-permute-done.9.other), custom_call_target="tpu_custom_call" | custom-call | tf_op jit(solution)/shard_map/pallas_call | solution.py:202
  128.4 2.1 %all-to-all-done.2.wide = bf16[8,128,128]{2,1,0:T(8,128)(2,1)S(1)} async-done(((bf16[8,128,128]{2,1,0:T(8,128)(2,1)}), bf16[8,128,128]{2,1,0:T(8,128)(2,1)S(1)}, u32[]{:S(2)}, u32[]{:S(2)}) %all-to-all-start.2) | async-done | bytes 262176 | tf_op jit(solution)/shard_map/all_to_all | solution.py:299
  130.5 35.4 %all_to_all.20.light = bf16[32,128,128]{2,1,0:T(8,128)(2,1)} all-to-all(bf16[32,128,128]{2,1,0:T(8,128)(2,1)} %shard_map.58), channel_id=1, replica_groups=mesh['clip'=4,'z'=8,'core'=2,'split'=4] {'z','split'}, dimensions={0} | all-to-all | bytes 2097152 | tf_op jit(solution)/shard_map/all_to_all | solution.py:261
  165.9 3.2 %shard_map.59 = bf16[128,4096]{1,0:T(8,128)(2,1)} custom-call(s32[32]{0:T(128)} %select_reduce_fusion.tab, bf16[8,128,128]{2,1,0:T(8,128)(2,1)} %copy-done.2, bf16[32,128,128]{2,1,0:T(8,128)(2,1)} %all_to_all.20.light), custom_call_target="tpu_custom_call" | custom-call | tf_op jit(solution)/shard_map/pallas_call | solution.py:202
  (37 shorter events, 3.4 us)
Async XLA Ops:
  1.9 11.5 %copy-start.4 = (s32[32]{0:T(128)S(1)}, s32[32]{0:T(128)}, u32[]{:S(2)}) copy-start(s32[32]{0:T(128)} %select_reduce_fusion.tab) | copy-start | bytes 388
  4.9 31.6 %all-to-all-start = ((bf16[8,3,128,128]{3,2,1,0:T(8,128)(2,1)}), bf16[8,3,128,128]{3,2,1,0:T(8,128)(2,1)S(1)}, u32[]{:S(2)}, u32[]{:S(2)}) async-start(bf16[8,3,128,128]{3,2,1,0:T(8,128)(2,1)} %shard_map.55), calls=%async_computation | async-start | bytes 1572864 | tf_op jit(solution)/shard_map/all_to_all | solution.py:266
  36.5 0.9 copy-start.1
  37.4 76.6 %all-to-all-start.1 = ((bf16[32,3,128,128]{3,2,1,0:T(8,128)(2,1)}), bf16[32,3,128,128]{3,2,1,0:T(8,128)(2,1)S(1)}, u32[]{:S(2)}, u32[]{:S(2)}) async-start(bf16[32,3,128,128]{3,2,1,0:T(8,128)(2,1)} %shard_map.56), calls=%async_computation.1 | async-start | bytes 6291456 | tf_op jit(solution)/shard_map/all_to_all | solution.py:261
  44.4 28.2 %collective-permute-start.1 = (bf16[2,8,128,128]{3,2,1,0:T(8,128)(2,1)}, bf16[2,8,128,128]{3,2,1,0:T(8,128)(2,1)}, u32[]{:S(2)}, u32[]{:S(2)}) collective-permute-start(bf16[2,8,128,128]{3,2,1,0:T(8,128)(2,1)} %slice_bitcast_fusion.refs_0_), channel_id=1, source_target_pairs={{0,3},{1,0},{2,1},{3,2},{4,7},{5,4},{6,5},{7,6},{8,11},{9,8},{10,9... | collective-permute-start | bytes 1572872 | tf_op jit(solution)/shard_map/ppermute | solution.py:273
  44.6 31.5 %collective-permute-start = (bf16[2,8,128,128]{3,2,1,0:T(8,128)(2,1)}, bf16[2,8,128,128]{3,2,1,0:T(8,128)(2,1)}, u32[]{:S(2)}, u32[]{:S(2)}) collective-permute-start(bf16[2,8,128,128]{3,2,1,0:T(8,128)(2,1)} %slice_bitcast_fusion.refs_0_), channel_id=1, source_target_pairs={{0,1},{1,2},{2,3},{3,0},{4,5},{5,6},{6,7},{7,4},{8,9},{9,10},{10,1... | collective-permute-start | bytes 1572872 | tf_op jit(solution)/shard_map/ppermute | solution.py:273
  46.4 39.1 %collective-permute-start.4 = (bf16[2,8,128,128]{3,2,1,0:T(8,128)(2,1)}, bf16[2,8,128,128]{3,2,1,0:T(8,128)(2,1)}, u32[]{:S(2)}, u32[]{:S(2)}) collective-permute-start(bf16[2,8,128,128]{3,2,1,0:T(8,128)(2,1)} %slice_bitcast_fusion.refs_0_), channel_id=1, source_target_pairs={{0,4},{4,0},{1,5},{5,1},{2,6},{6,2},{3,7},{7,3},{8,12},{12,8},{9,1... | collective-permute-start | bytes 1572872 | tf_op jit(solution)/shard_map/ppermute | solution.py:264
  73.6 10.6 %collective-permute-start.3 = (bf16[8,128,128]{2,1,0:T(8,128)(2,1)S(1)}, bf16[8,128,128]{2,1,0:T(8,128)(2,1)S(1)}, u32[]{:S(2)}, u32[]{:S(2)}) collective-permute-start(bf16[8,128,128]{2,1,0:T(8,128)(2,1)S(1)} %slice_bitcast_fusion.1), channel_id=1, source_target_pairs={{0,3},{1,0},{2,1},{3,2},{4,7},{5,4},{6,5},{7,6},{8,11},{9,8},{10,9... | collective-permute-start | bytes 786440 | tf_op jit(solution)/shard_map/ppermute | solution.py:273
  77.1 7.8 %collective-permute-start.2 = (bf16[8,128,128]{2,1,0:T(8,128)(2,1)S(1)}, bf16[8,128,128]{2,1,0:T(8,128)(2,1)}, u32[]{:S(2)}, u32[]{:S(2)}) collective-permute-start(bf16[8,128,128]{2,1,0:T(8,128)(2,1)S(1)} %slice_bitcast_fusion.2), channel_id=1, source_target_pairs={{0,1},{1,2},{2,3},{3,0},{4,5},{5,6},{6,7},{7,4},{8,9},{9,10},{10,1... | collective-permute-start | bytes 786440 | tf_op jit(solution)/shard_map/ppermute | solution.py:273
  77.3 9.5 %collective-permute-start.6 = (bf16[2,8,128,128]{3,2,1,0:T(8,128)(2,1)}, bf16[2,8,128,128]{3,2,1,0:T(8,128)(2,1)}, u32[]{:S(2)}, u32[]{:S(2)}) collective-permute-start(bf16[2,8,128,128]{3,2,1,0:T(8,128)(2,1)} %collective-permute-done.1.refs_2_), channel_id=1, source_target_pairs={{0,4},{4,0},{1,5},{5,1},{2,6},{6,2},{3,7},{7,3},{8,12},{12,8},{9,1... | collective-permute-start | bytes 1572872 | tf_op jit(solution)/shard_map/ppermute | solution.py:264
  77.3 9.5 %collective-permute-start.5 = (bf16[2,8,128,128]{3,2,1,0:T(8,128)(2,1)}, bf16[2,8,128,128]{3,2,1,0:T(8,128)(2,1)}, u32[]{:S(2)}, u32[]{:S(2)}) collective-permute-start(bf16[2,8,128,128]{3,2,1,0:T(8,128)(2,1)} %collective-permute-done.refs_1_), channel_id=1, source_target_pairs={{0,4},{4,0},{1,5},{5,1},{2,6},{6,2},{3,7},{7,3},{8,12},{12,8},{9,1... | collective-permute-start | bytes 1572872 | tf_op jit(solution)/shard_map/ppermute | solution.py:264
  84.2 2.5 %copy-start.3 = (bf16[8,128,128]{2,1,0:T(8,128)(2,1)}, bf16[8,128,128]{2,1,0:T(8,128)(2,1)S(1)}, u32[]{:S(2)}) copy-start(bf16[8,128,128]{2,1,0:T(8,128)(2,1)S(1)} %collective-permute-done.3.refs_4_) | copy-start | bytes 786436
  84.2 1.7 collective-permute-start.8
  84.9 1.9 %collective-permute-start.7 = (bf16[8,128,128]{2,1,0:T(8,128)(2,1)}, bf16[8,128,128]{2,1,0:T(8,128)(2,1)}, u32[]{:S(2)}, u32[]{:S(2)}) collective-permute-start(bf16[8,128,128]{2,1,0:T(8,128)(2,1)} %collective-permute-done.2.refs_3_), channel_id=1, source_target_pairs={{0,4},{4,0},{1,5},{5,1},{2,6},{6,2},{3,7},{7,3},{8,12},{12,8},{9,1... | collective-permute-start | bytes 786440 | tf_op jit(solution)/shard_map/ppermute | solution.py:264
  114.0 5.8 %copy-start = (bf16[32,3,128,128]{3,2,1,0:T(8,128)(2,1)}, bf16[32,3,128,128]{3,2,1,0:T(8,128)(2,1)S(1)}, u32[]{:S(2)}) copy-start(bf16[32,3,128,128]{3,2,1,0:T(8,128)(2,1)S(1)} %all-to-all-done.1.own) | copy-start | bytes 9437188
  114.0 5.8 %collective-permute-start.9 = (bf16[32,3,128,128]{3,2,1,0:T(8,128)(2,1)S(1)}, bf16[32,3,128,128]{3,2,1,0:T(8,128)(2,1)}, u32[]{:S(2)}, u32[]{:S(2)}) collective-permute-start(bf16[32,3,128,128]{3,2,1,0:T(8,128)(2,1)S(1)} %all-to-all-done.1.own), channel_id=1, source_target_pairs={{0,4},{4,0},{1,5},{5,1},{2,6},{6,2},{3,7},{7,3},{8,12},{12,8},{9,1... | collective-permute-start | bytes 9437192 | tf_op jit(solution)/shard_map/ppermute | solution.py:264
  114.0 16.6 %all-to-all-start.2 = ((bf16[8,128,128]{2,1,0:T(8,128)(2,1)}), bf16[8,128,128]{2,1,0:T(8,128)(2,1)S(1)}, u32[]{:S(2)}, u32[]{:S(2)}) async-start(bf16[8,128,128]{2,1,0:T(8,128)(2,1)} %shard_map.57), calls=%async_computation.2 | async-start | bytes 524288 | tf_op jit(solution)/shard_map/all_to_all | solution.py:299
  130.5 35.4 %copy-start.2 = (bf16[8,128,128]{2,1,0:T(8,128)(2,1)}, bf16[8,128,128]{2,1,0:T(8,128)(2,1)S(1)}, u32[]{:S(2)}) copy-start(bf16[8,128,128]{2,1,0:T(8,128)(2,1)S(1)} %all-to-all-done.2.wide) | copy-start | bytes 786436

commit v5 on v4

--- a/solution.py
+++ b/solution.py
@@ -265,7 +265,7 @@
 
     wide = lax.all_to_all(wide, "z", split_axis=0, concat_axis=0, tiled=True)
     wide, light, wide_lists, wide_counts, light_lists, light_counts = lax.optimization_barrier(
-        (wide, light, wide_lists, wide_counts, light_lists, light_counts)
+        (wide, light, wide_lists.reshape(-1), wide_counts, light_lists.reshape(-1), light_counts)
     )
     wide_kv = wide[:, 1:].transpose(1, 0, 2, 3)
 
@@ -297,9 +297,21 @@
         hbm=2,
     )[0]
     wide_out = lax.all_to_all(wide_out, "z", split_axis=0, concat_axis=0, tiled=True)
-    return local_call(
-        functools.partial(post_kernel, zs), [table], [wide_out, spread(light_out)], [queries.shape]
-    )[0]
+    half = BLOCK // 2
+    return pl.pallas_call(
+        functools.partial(post_kernel, zs),
+        out_shape=jax.ShapeDtypeStruct(queries.shape, jnp.bfloat16),
+        grid_spec=pltpu.PrefetchScalarGridSpec(
+            num_scalar_prefetch=1,
+            grid=(2,),
+            in_specs=[
+                pl.BlockSpec((zs, half, D), lambda i, *_: (0, i, 0)),
+                pl.BlockSpec((zs * ys, half, D), lambda i, *_: (0, i, 0)),
+            ],
+            out_specs=pl.BlockSpec((half, queries.shape[1]), lambda i, *_: (i, 0)),
+        ),
+        compiler_params=pltpu.CompilerParams(vmem_limit_bytes=56 * 2 ** 20),
+    )(table, wide_out, spread(light_out))
 
 
 def solution(mesh):

time: 170 us -> 169 us (level)
  local copies, waits for them, and re-layouts: 11.3 us -> 9.02 us
    pallas_call x5 -> x4, Pallas kernels: 36 us -> 32.8 us  [local_call(): pl.pallas_call(kernel, out_shape=[jax.ShapeDtypeStruct(x, jnp.bfloat16) f...]
    pallas_call x0 -> x1, Pallas kernels: none -> 2.91 us  [body(): pl.pallas_call(functools.partial(post_kernel, zs), out_shape=jax.ShapeDty...]
    squeeze x2, local copies, waits for them, and re-layouts: 1.94 us -> 0.04 us  [body(): parts = [wide_kv, before, after, over_y(before[0], 1), over_y(after[1], -1)]]
  transfers between devices with their start and end apart: 13 -> 13, of which waited for: 9 -> 9; matrix products, arithmetic and copies ran while one was open for 6% -> 5% of each run, Pallas kernels for 18% -> 18%
where the time goes in v5:
time: 169 us; the launch traced here: 168 us
  waiting for transfers between devices  57.7 us (34%)
  Pallas kernels  35.7 us (21%)
  blocking collectives  34.8 us (21%)
  starting transfers between devices  23.9 us (14%)
  local copies, waits for them, and re-layouts  9.02 us (5%)
  other arithmetic  3.7 us (2%)
  between operations  3.53 us (2%)
    all_to_all x1, blocking collectives, spread(): lax.all_to_all(x, ('z', 'split'), split_axis=0, concat_axis=0, tiled=True)  34.8 us
    ppermute x4, waiting for transfers between devices, over_y(): return lax.ppermute(x, 'split', [(i, (i + dy) % ys) for i in range(ys)])  33.4 us
    pallas_call x4, Pallas kernels, local_call(): pl.pallas_call(kernel, out_shape=[jax.ShapeDtypeStruct(x, jnp.bfloat16) f...  32.8 us
    all_to_all x1, waiting for transfers between devices, spread(): lax.all_to_all(x, ('z', 'split'), split_axis=0, concat_axis=0, tiled=True)  11 us
    all_to_all x1, starting transfers between devices, body(): wide = lax.all_to_all(wide, 'z', split_axis=0, concat_axis=0, tiled=True)  8.48 us
    all_to_all x1, waiting for transfers between devices, body(): wide = lax.all_to_all(wide, 'z', split_axis=0, concat_axis=0, tiled=True)  7.87 us
    ppermute x4, starting transfers between devices, over_y(): return lax.ppermute(x, 'split', [(i, (i + dy) % ys) for i in range(ys)])  5.78 us
    all_to_all x1, starting transfers between devices, spread(): lax.all_to_all(x, ('z', 'split'), split_axis=0, concat_axis=0, tiled=True)  5.08 us
  transfers between devices with their start and end apart: 13, of which 9 were waited for; matrix products, arithmetic and copies ran while one was open for 5% of the time, Pallas kernels for 18%

profile of v5, /device:TPU:12, one launch (start us, length us, event | category | flops | bytes accessed | tf_op | source)
XLA Modules:
  0.0 168.3 jit_solution(18112915576644774680)
XLA Ops:
  0.0 0.8 reduce_sum.27
  1.2 0.8 select_reduce_fusion.tab
  2.0 3.0 %shard_map.55 = bf16[8,3,128,128]{3,2,1,0:T(8,128)(2,1)} custom-call(s32[32]{0:T(128)} %select_reduce_fusion.tab, bf16[128,4096]{1,0:T(8,128)(2,1)} %q_ref.3, bf16[128,4096]{1,0:T(8,128)(2,1)} %k_ref.3, bf16[128,4096]{1,0:T(8,128)(2,1)} %v_ref.3), custom_call_target="tpu_custom_call" | custom-call | tf_op jit(solution)/shard_map/pallas_call | solution.py:202
  5.0 8.5 %all-to-all-start = ((bf16[8,3,128,128]{3,2,1,0:T(8,128)(2,1)}), bf16[8,3,128,128]{3,2,1,0:T(8,128)(2,1)S(1)}, u32[]{:S(2)}, u32[]{:S(2)}) async-start(bf16[8,3,128,128]{3,2,1,0:T(8,128)(2,1)} %shard_map.55), calls=%async_computation | async-start | bytes 1572864 | tf_op jit(solution)/shard_map/all_to_all | solution.py:266
  16.2 4.8 %shard_map.56 = bf16[32,3,128,128]{3,2,1,0:T(8,128)(2,1)} custom-call(s32[32]{0:T(128)} %select_reduce_fusion.tab, bf16[128,4096]{1,0:T(8,128)(2,1)} %q_ref.3, bf16[128,4096]{1,0:T(8,128)(2,1)} %k_ref.3, bf16[128,4096]{1,0:T(8,128)(2,1)} %v_ref.3), custom_call_target="tpu_custom_call" | custom-call | tf_op jit(solution)/shard_map/pallas_call | solution.py:202
  22.1 0.7 fusion.27
  22.9 0.7 gather_fusion.3
  23.6 0.8 dynamic-slice_bitcast_fusion
  25.0 1.2 gather_fusion.1
  27.5 0.6 fusion.20.lists
  28.1 0.6 fusion.7.lists
  28.7 7.9 %all-to-all-done.q_hbm = bf16[8,3,128,128]{3,2,1,0:T(8,128)(2,1)S(1)} async-done(((bf16[8,3,128,128]{3,2,1,0:T(8,128)(2,1)}), bf16[8,3,128,128]{3,2,1,0:T(8,128)(2,1)S(1)}, u32[]{:S(2)}, u32[]{:S(2)}) %all-to-all-start) | async-done | bytes 786464 | tf_op jit(solution)/shard_map/all_to_all | solution.py:266
  36.6 0.9 copy-done.1
  37.4 5.1 %all-to-all-start.1 = ((bf16[32,3,128,128]{3,2,1,0:T(8,128)(2,1)}), bf16[32,3,128,128]{3,2,1,0:T(8,128)(2,1)S(1)}, u32[]{:S(2)}, u32[]{:S(2)}) async-start(bf16[32,3,128,128]{3,2,1,0:T(8,128)(2,1)} %shard_map.56), calls=%async_computation.1 | async-start | bytes 6291456 | tf_op jit(solution)/shard_map/all_to_all | solution.py:261
  42.5 1.1 slice_bitcast_fusion.refs_0_
  43.9 1.8 %collective-permute-start = (bf16[2,8,128,128]{3,2,1,0:T(8,128)(2,1)S(1)}, bf16[2,8,128,128]{3,2,1,0:T(8,128)(2,1)S(1)}, u32[]{:S(2)}, u32[]{:S(2)}) collective-permute-start(bf16[2,8,128,128]{3,2,1,0:T(8,128)(2,1)S(1)} %slice_bitcast_fusion.refs_0_), channel_id=1, source_target_pairs={{0,1},{1,2},{2,3},{3,0},{4,5},{5,6},{6,7},{7,4},{8,9},{9,10},{10,1... | collective-permute-start | bytes 1572872 | tf_op jit(solution)/shard_map/ppermute | solution.py:273
  45.7 26.8 %collective-permute-done.1.refs_2_ = bf16[2,8,128,128]{3,2,1,0:T(8,128)(2,1)S(1)} collective-permute-done((bf16[2,8,128,128]{3,2,1,0:T(8,128)(2,1)S(1)}, bf16[2,8,128,128]{3,2,1,0:T(8,128)(2,1)S(1)}, u32[]{:S(2)}, u32[]{:S(2)}) %collective-permute-start.1) | collective-permute-done | bytes 524320 | tf_op jit(solution)/shard_map/ppermute | solution.py:273
  72.5 2.5 %collective-permute-start.3 = (bf16[8,128,128]{2,1,0:T(8,128)(2,1)S(1)}, bf16[8,128,128]{2,1,0:T(8,128)(2,1)S(1)}, u32[]{:S(2)}, u32[]{:S(2)}) collective-permute-start(bf16[8,128,128]{2,1,0:T(8,128)(2,1)S(1)} %slice_bitcast_fusion.1), channel_id=1, source_target_pairs={{0,3},{1,0},{2,1},{3,2},{4,7},{5,4},{6,5},{7,6},{8,11},{9,8},{10,9... | collective-permute-start | bytes 786440 | tf_op jit(solution)/shard_map/ppermute | solution.py:273
  75.1 1.1 collective-permute-start.2
  76.8 5.3 %collective-permute-done.3.refs_4_ = bf16[8,128,128]{2,1,0:T(8,128)(2,1)S(1)} collective-permute-done((bf16[8,128,128]{2,1,0:T(8,128)(2,1)S(1)}, bf16[8,128,128]{2,1,0:T(8,128)(2,1)S(1)}, u32[]{:S(2)}, u32[]{:S(2)}) %collective-permute-start.3) | collective-permute-done | bytes 262176 | tf_op jit(solution)/shard_map/ppermute | solution.py:273
  82.1 1.2 collective-permute-done.2.refs_3_
  83.6 1.2 collective-permute-done.7.refs_8_
  85.0 0.6 copy-done.12
  85.8 0.8 copy-done.8
  86.6 16.4 %shard_map.57 = bf16[8,128,128]{2,1,0:T(8,128)(2,1)} custom-call(s32[512]{0:T(512)} %fusion.20.lists, s32[8]{0:T(128)} %gather_fusion.1, bf16[8,3,128,128]{3,2,1,0:T(8,128)(2,1)} %copy-done.1, bf16[2,8,128,128]{3,2,1,0:T(8,128)(2,1)} %copy-done.2, bf16[2,8,128,128]{3,2,1,0:T(8,128)(2,1)} %copy-done.4, bf16[2,8,128,128]{3,2,1,0:T(8,128)(2,1)} %copy-done.3, ...), custom_call_target="tpu_custom_call" | custom-call | tf_op jit(solution)/shard_map/pallas_call | solution.py:202
  103.0 11.0 %all-to-all-done.1.own = bf16[32,3,128,128]{3,2,1,0:T(8,128)(2,1)S(1)} async-done(((bf16[32,3,128,128]{3,2,1,0:T(8,128)(2,1)}), bf16[32,3,128,128]{3,2,1,0:T(8,128)(2,1)S(1)}, u32[]{:S(2)}, u32[]{:S(2)}) %all-to-all-start.1) | async-done | bytes 3145760 | tf_op jit(solution)/shard_map/all_to_all | solution.py:261
  114.0 4.0 %all-to-all-start.2 = ((bf16[8,128,128]{2,1,0:T(8,128)(2,1)}), bf16[8,128,128]{2,1,0:T(8,128)(2,1)S(1)}, u32[]{:S(2)}, u32[]{:S(2)}) async-start(bf16[8,128,128]{2,1,0:T(8,128)(2,1)} %shard_map.57), calls=%async_computation.2 | async-start | bytes 524288 | tf_op jit(solution)/shard_map/all_to_all | solution.py:299
  118.0 1.8 %collective-permute-done.9.other = bf16[32,3,128,128]{3,2,1,0:T(8,128)(2,1)} collective-permute-done((bf16[32,3,128,128]{3,2,1,0:T(8,128)(2,1)S(1)}, bf16[32,3,128,128]{3,2,1,0:T(8,128)(2,1)}, u32[]{:S(2)}, u32[]{:S(2)}) %collective-permute-start.9) | collective-permute-done | bytes 3145760 | tf_op jit(solution)/shard_map/ppermute | solution.py:264
  119.8 8.6 %shard_map.58 = bf16[32,128,128]{2,1,0:T(8,128)(2,1)} custom-call(s32[2048]{0:T(1024)} %fusion.7.lists, s32[32]{0:T(128)} %broadcast_select_fusion.counts, bf16[32,3,128,128]{3,2,1,0:T(8,128)(2,1)} %copy-done, bf16[32,3,128,128]{3,2,1,0:T(8,128)(2,1)} %collective-permute-done.9.other), custom_call_target="tpu_custom_call" | custom-call | tf_op jit(solution)/shard_map/pallas_call | solution.py:202
  128.4 2.1 %all-to-all-done.2.wide = bf16[8,128,128]{2,1,0:T(8,128)(2,1)S(1)} async-done(((bf16[8,128,128]{2,1,0:T(8,128)(2,1)}), bf16[8,128,128]{2,1,0:T(8,128)(2,1)S(1)}, u32[]{:S(2)}, u32[]{:S(2)}) %all-to-all-start.2) | async-done | bytes 262176 | tf_op jit(solution)/shard_map/all_to_all | solution.py:299
  130.6 34.8 %all_to_all.20.light = bf16[32,128,128]{2,1,0:T(8,128)(2,1)} all-to-all(bf16[32,128,128]{2,1,0:T(8,128)(2,1)} %shard_map.58), channel_id=1, replica_groups=mesh['clip'=4,'z'=8,'core'=2,'split'=4] {'z','split'}, dimensions={0} | all-to-all | bytes 2097152 | tf_op jit(solution)/shard_map/all_to_all | solution.py:261
  165.4 2.9 %shard_map.59 = bf16[128,4096]{1,0:T(8,128)(2,1)} custom-call(s32[32]{0:T(128)} %select_reduce_fusion.tab, bf16[8,128,128]{2,1,0:T(8,128)(2,1)} %copy-done.5, bf16[32,128,128]{2,1,0:T(8,128)(2,1)} %all_to_all.20.light), custom_call_target="tpu_custom_call" | custom-call | tf_op jit(solution)/shard_map/pallas_call | solution.py:301
  (55 shorter events, 4.2 us)
Async XLA Ops:
  2.0 11.5 %copy-start.13 = (s32[32]{0:T(128)S(1)}, s32[32]{0:T(128)}, u32[]{:S(2)}) copy-start(s32[32]{0:T(128)} %select_reduce_fusion.tab) | copy-start | bytes 388
  5.0 31.6 %all-to-all-start = ((bf16[8,3,128,128]{3,2,1,0:T(8,128)(2,1)}), bf16[8,3,128,128]{3,2,1,0:T(8,128)(2,1)S(1)}, u32[]{:S(2)}, u32[]{:S(2)}) async-start(bf16[8,3,128,128]{3,2,1,0:T(8,128)(2,1)} %shard_map.55), calls=%async_computation | async-start | bytes 1572864 | tf_op jit(solution)/shard_map/all_to_all | solution.py:266
  36.5 0.9 copy-start.1
  37.4 76.6 %all-to-all-start.1 = ((bf16[32,3,128,128]{3,2,1,0:T(8,128)(2,1)}), bf16[32,3,128,128]{3,2,1,0:T(8,128)(2,1)S(1)}, u32[]{:S(2)}, u32[]{:S(2)}) async-start(bf16[32,3,128,128]{3,2,1,0:T(8,128)(2,1)} %shard_map.56), calls=%async_computation.1 | async-start | bytes 6291456 | tf_op jit(solution)/shard_map/all_to_all | solution.py:261
  43.6 41.3 %copy-start.2 = (bf16[2,8,128,128]{3,2,1,0:T(8,128)(2,1)}, bf16[2,8,128,128]{3,2,1,0:T(8,128)(2,1)S(1)}, u32[]{:S(2)}) copy-start(bf16[2,8,128,128]{3,2,1,0:T(8,128)(2,1)S(1)} %slice_bitcast_fusion.refs_0_) | copy-start | bytes 1572868
  43.6 28.9 %collective-permute-start.1 = (bf16[2,8,128,128]{3,2,1,0:T(8,128)(2,1)S(1)}, bf16[2,8,128,128]{3,2,1,0:T(8,128)(2,1)S(1)}, u32[]{:S(2)}, u32[]{:S(2)}) collective-permute-start(bf16[2,8,128,128]{3,2,1,0:T(8,128)(2,1)S(1)} %slice_bitcast_fusion.refs_0_), channel_id=1, source_target_pairs={{0,3},{1,0},{2,1},{3,2},{4,7},{5,4},{6,5},{7,6},{8,11},{9,8},{10,9... | collective-permute-start | bytes 1572872 | tf_op jit(solution)/shard_map/ppermute | solution.py:273
  43.9 31.2 %collective-permute-start = (bf16[2,8,128,128]{3,2,1,0:T(8,128)(2,1)S(1)}, bf16[2,8,128,128]{3,2,1,0:T(8,128)(2,1)S(1)}, u32[]{:S(2)}, u32[]{:S(2)}) collective-permute-start(bf16[2,8,128,128]{3,2,1,0:T(8,128)(2,1)S(1)} %slice_bitcast_fusion.refs_0_), channel_id=1, source_target_pairs={{0,1},{1,2},{2,3},{3,0},{4,5},{5,6},{6,7},{7,4},{8,9},{9,10},{10,1... | collective-permute-start | bytes 1572872 | tf_op jit(solution)/shard_map/ppermute | solution.py:273
  45.7 37.6 %collective-permute-start.4 = (bf16[2,8,128,128]{3,2,1,0:T(8,128)(2,1)S(1)}, bf16[2,8,128,128]{3,2,1,0:T(8,128)(2,1)S(1)}, u32[]{:S(2)}, u32[]{:S(2)}) collective-permute-start(bf16[2,8,128,128]{3,2,1,0:T(8,128)(2,1)S(1)} %slice_bitcast_fusion.refs_0_), channel_id=1, source_target_pairs={{0,4},{4,0},{1,5},{5,1},{2,6},{6,2},{3,7},{7,3},{8,12},{12,8},{9,1... | collective-permute-start | bytes 1572872 | tf_op jit(solution)/shard_map/ppermute | solution.py:264
  72.5 12.4 %copy-start.3 = (bf16[2,8,128,128]{3,2,1,0:T(8,128)(2,1)}, bf16[2,8,128,128]{3,2,1,0:T(8,128)(2,1)S(1)}, u32[]{:S(2)}) copy-start(bf16[2,8,128,128]{3,2,1,0:T(8,128)(2,1)S(1)} %collective-permute-done.1.refs_2_) | copy-start | bytes 1572868
  72.5 9.6 %collective-permute-start.3 = (bf16[8,128,128]{2,1,0:T(8,128)(2,1)S(1)}, bf16[8,128,128]{2,1,0:T(8,128)(2,1)S(1)}, u32[]{:S(2)}, u32[]{:S(2)}) collective-permute-start(bf16[8,128,128]{2,1,0:T(8,128)(2,1)S(1)} %slice_bitcast_fusion.1), channel_id=1, source_target_pairs={{0,3},{1,0},{2,1},{3,2},{4,7},{5,4},{6,5},{7,6},{8,11},{9,8},{10,9... | collective-permute-start | bytes 786440 | tf_op jit(solution)/shard_map/ppermute | solution.py:273
  75.1 9.8 %copy-start.4 = (bf16[2,8,128,128]{3,2,1,0:T(8,128)(2,1)}, bf16[2,8,128,128]{3,2,1,0:T(8,128)(2,1)S(1)}, u32[]{:S(2)}) copy-start(bf16[2,8,128,128]{3,2,1,0:T(8,128)(2,1)S(1)} %collective-permute-done.refs_1_) | copy-start | bytes 1572868
  75.1 8.2 %collective-permute-start.2 = (bf16[8,128,128]{2,1,0:T(8,128)(2,1)S(1)}, bf16[8,128,128]{2,1,0:T(8,128)(2,1)S(1)}, u32[]{:S(2)}, u32[]{:S(2)}) collective-permute-start(bf16[8,128,128]{2,1,0:T(8,128)(2,1)S(1)} %slice_bitcast_fusion.2), channel_id=1, source_target_pairs={{0,1},{1,2},{2,3},{3,0},{4,5},{5,6},{6,7},{7,4},{8,9},{9,10},{10,1... | collective-permute-start | bytes 786440 | tf_op jit(solution)/shard_map/ppermute | solution.py:273
  76.3 8.6 %collective-permute-start.6 = (bf16[2,8,128,128]{3,2,1,0:T(8,128)(2,1)S(1)}, bf16[2,8,128,128]{3,2,1,0:T(8,128)(2,1)S(1)}, u32[]{:S(2)}, u32[]{:S(2)}) collective-permute-start(bf16[2,8,128,128]{3,2,1,0:T(8,128)(2,1)S(1)} %collective-permute-done.1.refs_2_), channel_id=1, source_target_pairs={{0,4},{4,0},{1,5},{5,1},{2,6},{6,2},{3,7},{7,3},{8,12},{12,8},{9,1... | collective-permute-start | bytes 1572872 | tf_op jit(solution)/shard_map/ppermute | solution.py:264
  76.3 8.7 %collective-permute-start.5 = (bf16[2,8,128,128]{3,2,1,0:T(8,128)(2,1)S(1)}, bf16[2,8,128,128]{3,2,1,0:T(8,128)(2,1)S(1)}, u32[]{:S(2)}, u32[]{:S(2)}) collective-permute-start(bf16[2,8,128,128]{3,2,1,0:T(8,128)(2,1)S(1)} %collective-permute-done.refs_1_), channel_id=1, source_target_pairs={{0,4},{4,0},{1,5},{5,1},{2,6},{6,2},{3,7},{7,3},{8,12},{12,8},{9,1... | collective-permute-start | bytes 1572872 | tf_op jit(solution)/shard_map/ppermute | solution.py:264
  82.1 2.8 %copy-start.9 = (bf16[8,128,128]{2,1,0:T(8,128)(2,1)}, bf16[8,128,128]{2,1,0:T(8,128)(2,1)S(1)}, u32[]{:S(2)}) copy-start(bf16[8,128,128]{2,1,0:T(8,128)(2,1)S(1)} %collective-permute-done.3.refs_4_) | copy-start | bytes 786436
  82.1 1.5 collective-permute-start.8
  83.4 1.6 copy-start.10
  83.4 1.5 collective-permute-start.7
  83.4 1.6 copy-start.6
  83.6 1.3 copy-start.11
  84.9 0.7 copy-start.12
  84.9 0.9 copy-start.7
  85.8 0.8 copy-start.8
  114.0 5.8 %copy-start = (bf16[32,3,128,128]{3,2,1,0:T(8,128)(2,1)}, bf16[32,3,128,128]{3,2,1,0:T(8,128)(2,1)S(1)}, u32[]{:S(2)}) copy-start(bf16[32,3,128,128]{3,2,1,0:T(8,128)(2,1)S(1)} %all-to-all-done.1.own) | copy-start | bytes 9437188
  114.0 5.8 %collective-permute-start.9 = (bf16[32,3,128,128]{3,2,1,0:T(8,128)(2,1)S(1)}, bf16[32,3,128,128]{3,2,1,0:T(8,128)(2,1)}, u32[]{:S(2)}, u32[]{:S(2)}) collective-permute-start(bf16[32,3,128,128]{3,2,1,0:T(8,128)(2,1)S(1)} %all-to-all-done.1.own), channel_id=1, source_target_pairs={{0,4},{4,0},{1,5},{5,1},{2,6},{6,2},{3,7},{7,3},{8,12},{12,8},{9,1... | collective-permute-start | bytes 9437192 | tf_op jit(solution)/shard_map/ppermute | solution.py:264
  114.0 16.6 %all-to-all-start.2 = ((bf16[8,128,128]{2,1,0:T(8,128)(2,1)}), bf16[8,128,128]{2,1,0:T(8,128)(2,1)S(1)}, u32[]{:S(2)}, u32[]{:S(2)}) async-start(bf16[8,128,128]{2,1,0:T(8,128)(2,1)} %shard_map.57), calls=%async_computation.2 | async-start | bytes 524288 | tf_op jit(solution)/shard_map/all_to_all | solution.py:299
  130.6 34.8 %copy-start.5 = (bf16[8,128,128]{2,1,0:T(8,128)(2,1)}, bf16[8,128,128]{2,1,0:T(8,128)(2,1)S(1)}, u32[]{:S(2)}) copy-start(bf16[8,128,128]{2,1,0:T(8,128)(2,1)S(1)} %all-to-all-done.2.wide) | copy-start | bytes 786436
